TPU v7x, 128 devices: a whole 4x4x4 slice. The times are simulated.
128 devices in a mesh: row: 32 (over x, z, y_hi), col: 4 (over y_lo, core).
Axes of the slice: x: 4, y: 4 (y_hi: 2, y_lo: 2; y = y_hi * 2 + y_lo), z: 4, core: 2. Of those that a mesh axis runs over, the one named last changes fastest.
Arguments:
- counts: int32 [3, 32768, 4096], P(None, 'row', 'col'), may hold values from 0 to 255, as said below
- row_embed: float32 [32768, 256], P('row'), may hold values from -1.5 to 1.5
- row_accum: float32 [32768, 256], P('row'), may hold values from 0.5 to 4
- col_embed: float32 [4096, 256], P('col'), may hold values from -1.5 to 1.5
- col_accum: float32 [4096, 256], P('col'), may hold values from 0.5 to 4
- row_log: float32 [32768], P('row'), may hold values from -4 to 4
- col_log: float32 [4096], P('col'), may hold values from -4 to 4
Outputs:
- row_embed_out: float32 [32768, 256], P('row')
- row_accum_out: float32 [32768, 256], P('row')
- col_embed_out: float32 [4096, 256], P('col')
- col_accum_out: float32 [4096, 256], P('col')
Inputs may be any that keep to these rules, and one draw needn't show every extreme that they name: About a third of the counts are zero; 255 is reached.
All inputs are finite; a program needn't handle non-finite values.
Results may differ from a plain program's by a relative error of at most 0.0003.
Values sent between devices are 32-bit elements; how exact they have to be, the bound alone decides.
No kernel may reach another device: no remote copies, remote signals or barrier semaphores. Data moves between devices by JAX's collectives and lax.ppermute only.
A program may use at most 128 MiB of HBM per device.

v0:
```python
import math

import jax
import jax.numpy as jnp
from jax import lax
from jax.sharding import PartitionSpec as P

highest = lax.Precision.HIGHEST
learn_rate = 0.5


def passed_along(block, axis, distance):
    devices = range(lax.axis_size(axis))
    route = [((i - distance) % len(devices), i) for i in devices]
    return lax.ppermute(block, axis, route)


def swivel_residual(block, row_vecs, col_vecs, row_bias, col_bias):
    values = block.astype(jnp.float32)
    scores = jnp.dot(row_vecs, col_vecs.T, precision=highest, preferred_element_type=jnp.float32)
    base = -(row_bias[:, None] + col_bias[None, :])
    target = jnp.log(jnp.maximum(values, 1.0)) + base
    confidence = 0.1 + 0.25 * jnp.sqrt(values)
    return jnp.where(block > 0, confidence * (scores - target), jax.nn.sigmoid(scores - base))


def adagrad(vecs, sums, grad):
    new_sums = sums + grad * grad
    return (vecs - learn_rate * grad / jnp.sqrt(new_sums), new_sums)


def shards(counts, row_embed, row_accum, col_embed, col_accum, row_log, col_log):
    row_vecs, row_sums, row_bias = (row_embed, row_accum, row_log)
    col_vecs, col_sums, col_bias = (col_embed, col_accum, col_log)
    n_row = lax.axis_size("row")
    n_col = lax.axis_size("col")
    row_scale = math.sqrt(n_col * col_vecs.shape[0])
    col_scale = math.sqrt(n_row * row_vecs.shape[0])
    turns = counts.shape[0]
    for turn in range(turns):
        if turn > 0:
            col_vecs, col_sums, col_bias = passed_along((col_vecs, col_sums, col_bias), "col", 1)
        residual = swivel_residual(counts[turn], row_vecs, col_vecs, row_bias, col_bias)
        row_part = jnp.dot(
            residual, col_vecs, precision=highest, preferred_element_type=jnp.float32
        )
        product = lax.dot_general(
            residual,
            row_vecs,
            (((0,), (0,)), ((), ())),
            precision=highest,
            preferred_element_type=jnp.float32,
        )
        row_total = lax.psum(row_part, "col")
        row_vecs, row_sums = adagrad(row_vecs, row_sums, row_total / row_scale)
        col_total = lax.psum(product, "row")
        col_vecs, col_sums = adagrad(col_vecs, col_sums, col_total / col_scale)
    return (row_vecs, row_sums, col_vecs, col_sums)


def solution(mesh):
    return jax.shard_map(
        shards,
        mesh=mesh,
        in_specs=(
            P(None, "row", "col"),
            P("row", None),
            P("row", None),
            P("col", None),
            P("col", None),
            P("row"),
            P("col"),
        ),
        out_specs=(P("row", None), P("row", None), P("col", None), P("col", None)),
        check_vma=False,
    )
```

profile of v0, /device:TPU:8, one launch (start us, length us, event | category | flops | bytes accessed | tf_op | source)
XLA Modules:
  0.0 1280.2 jit_solution(3791313482753158897)
XLA Ops:
  7.2 9.9 fusion.8
  17.1 1.9 copy-done.1
  19.0 8.0 fusion.11
  27.1 6.6 fusion.10
  33.8 348.2 %all-reduce.9.cloned.1.call-done = f32[1024,256]{1,0:T(8,128)} async-done(((f32[1024,256]{1,0:T(8,128)}), f32[1024,256]{1,0:T(8,128)}) %all-reduce.9.cloned.1.call-update) | async-done | bytes 1048592 | tf_op jit(solution)/shard_map/psum | solution.py:56
  381.9 3.1 multiply_add_fusion.4
  385.6 22.4 %collective-permute-done.1 = f32[1024]{0:T(1024)S(1)} collective-permute-done((f32[1024]{0:T(1024)S(1)}, f32[1024]{0:T(1024)S(1)}, u32[]{:S(2)}, u32[]{:S(2)}) %collective-permute-start.1) | collective-permute-done | bytes 4128 | tf_op jit(solution)/shard_map/ppermute | solution.py:15
  408.0 20.9 %all-reduce.7.cloned.1.call-done = f32[1024,256]{1,0:T(8,128)} async-done(((f32[1024,256]{1,0:T(8,128)}), f32[1024,256]{1,0:T(8,128)}) %all-reduce.7.cloned.1.call-update) | async-done | bytes 1048592 | tf_op jit(solution)/shard_map/psum | solution.py:54
  428.9 10.0 fusion.5
  439.0 1.9 copy-done.2
  440.9 8.2 fusion.9
  449.4 6.9 fusion.12
  456.4 8.0 collective-permute-done.2
  464.4 338.7 %all-reduce.13.cloned.1.call-done = f32[1024,256]{1,0:T(8,128)} async-done(((f32[1024,256]{1,0:T(8,128)}), f32[1024,256]{1,0:T(8,128)}) %all-reduce.13.cloned.1.call-update) | async-done | bytes 1048592 | tf_op jit(solution)/shard_map/psum | solution.py:56
  803.1 3.1 multiply_add_fusion.2
  807.1 43.0 %all-reduce.11.cloned.1.call-done = f32[1024,256]{1,0:T(8,128)} async-done(((f32[1024,256]{1,0:T(8,128)}), f32[1024,256]{1,0:T(8,128)}) %all-reduce.11.cloned.1.call-update) | async-done | bytes 1048592 | tf_op jit(solution)/shard_map/psum | solution.py:54
  850.1 2.0 multiply_subtract_fusion.3
  852.1 8.8 fusion.2
  862.9 5.6 fusion.13
  869.0 9.9 fusion.14
  879.0 34.5 %all-reduce.15.cloned.1.call-done = f32[1024,256]{1,0:T(8,128)} async-done(((f32[1024,256]{1,0:T(8,128)}), f32[1024,256]{1,0:T(8,128)}) %all-reduce.15.cloned.1.call-update) | async-done | bytes 1048592 | tf_op jit(solution)/shard_map/psum | solution.py:54
  913.5 3.3 multiply_subtract_fusion.1
  916.8 353.0 %all-reduce.17.cloned.1.call-done = f32[1024,256]{1,0:T(8,128)} async-done(((f32[1024,256]{1,0:T(8,128)}), f32[1024,256]{1,0:T(8,128)}) %all-reduce.17.cloned.1.call-update) | async-done | bytes 1048592 | tf_op jit(solution)/shard_map/psum | solution.py:56
  1269.7 3.4 multiply_subtract_fusion
  (38 shorter events, 4.5 us)
Async XLA Ops:
  7.2 11.9 copy-start.5
  7.2 374.8 %all-reduce.9.cloned.1.call-start = ((), (), s32[]{:S(2)}) async-start(), calls=%async_computation.1 | async-start | bytes 2097152 | tf_op jit(solution)/shard_map/psum | solution.py:56
  17.1 2.0 copy-start.1
  19.0 8.1 copy-start.6
  27.1 401.9 %all-reduce.7.cloned.1.call-start = ((), (), s32[]{:S(2)}) async-start(), calls=%async_computation | async-start | bytes 2097152 | tf_op jit(solution)/shard_map/psum | solution.py:54
  33.7 351.3 %copy-start.7 = (f32[1024]{0:T(1024)S(1)}, f32[1024]{0:T(1024)}, u32[]{:S(2)}) copy-start(f32[1024]{0:T(1024)} %param.13) | copy-start | bytes 12292
  33.7 395.2 %copy-start.3 = (f32[1024,256]{1,0:T(8,128)S(1)}, f32[1024,256]{1,0:T(8,128)}, u32[]{:S(2)}) copy-start(f32[1024,256]{1,0:T(8,128)} %param.9) | copy-start | bytes 3145732
  33.7 395.2 %copy-start.8 = (f32[1024]{0:T(1024)S(1)}, f32[1024]{0:T(1024)}, u32[]{:S(2)}) copy-start(f32[1024]{0:T(1024)} %param.12) | copy-start | bytes 12292
  33.7 769.3 %all-reduce.13.cloned.1.call-start = ((), (), s32[]{:S(2)}) async-start(), calls=%async_computation.3 | async-start | bytes 2097152 | tf_op jit(solution)/shard_map/psum | solution.py:56
  385.0 43.9 %collective-permute-start = (f32[1024,256]{1,0:T(8,128)}, f32[1024,256]{1,0:T(8,128)}, u32[]{:S(2)}, u32[]{:S(2)}) collective-permute-start(f32[1024,256]{1,0:T(8,128)} %get-tuple-element.11), channel_id=1, source_target_pairs={{3,0},{0,1},{1,2},{2,3},{7,4},{4,5},{5,6},{6,7},{11,8},{8,9},{9,10... | collective-permute-start | bytes 3145736 | tf_op jit(solution)/shard_map/ppermute | solution.py:15
  385.1 23.0 %collective-permute-start.1 = (f32[1024]{0:T(1024)S(1)}, f32[1024]{0:T(1024)S(1)}, u32[]{:S(2)}, u32[]{:S(2)}) collective-permute-start(f32[1024]{0:T(1024)S(1)} %copy-done.7), channel_id=1, source_target_pairs={{3,0},{0,1},{1,2},{2,3},{7,4},{4,5},{5,6},{6,7},{11,8},{8,9},{9,10... | collective-permute-start | bytes 12296 | tf_op jit(solution)/shard_map/ppermute | solution.py:15
  428.9 12.0 copy-start.4
  439.0 2.0 copy-start.2
  449.1 401.0 %all-reduce.11.cloned.1.call-start = ((), (), s32[]{:S(2)}) async-start(), calls=%async_computation.2 | async-start | bytes 2097152 | tf_op jit(solution)/shard_map/psum | solution.py:54
  449.1 15.2 %collective-permute-start.2 = (f32[1024,256]{1,0:T(8,128)}, f32[1024,256]{1,0:T(8,128)S(1)}, u32[]{:S(2)}, u32[]{:S(2)}) collective-permute-start(f32[1024,256]{1,0:T(8,128)} %get-tuple-element.10), channel_id=1, source_target_pairs={{3,0},{0,1},{1,2},{2,3},{7,4},{4,5},{5,6},{6,7},{11,8},{8,9},{9,10... | collective-permute-start | bytes 3145736 | tf_op jit(solution)/shard_map/ppermute | solution.py:15
  456.3 457.1 %all-reduce.15.cloned.1.call-start = ((), (), s32[]{:S(2)}) async-start(), calls=%async_computation.4 | async-start | bytes 2097152 | tf_op jit(solution)/shard_map/psum | solution.py:54
  806.2 45.9 %collective-permute-start.3 = (f32[1024,256]{1,0:T(8,128)}, f32[1024,256]{1,0:T(8,128)}, u32[]{:S(2)}, u32[]{:S(2)}) collective-permute-start(f32[1024,256]{1,0:T(8,128)} %get-tuple-element.9), channel_id=1, source_target_pairs={{3,0},{0,1},{1,2},{2,3},{7,4},{4,5},{5,6},{6,7},{11,8},{8,9},{9,10... | collective-permute-start | bytes 3145736 | tf_op jit(solution)/shard_map/ppermute | solution.py:15
  806.2 45.9 %collective-permute-start.4 = (f32[1024]{0:T(1024)S(1)}, f32[1024]{0:T(1024)S(1)}, u32[]{:S(2)}, u32[]{:S(2)}) collective-permute-start(f32[1024]{0:T(1024)S(1)} %collective-permute-done.1), channel_id=1, source_target_pairs={{3,0},{0,1},{1,2},{2,3},{7,4},{4,5},{5,6},{6,7},{11,8},{8,9},{9,10... | collective-permute-start | bytes 12296 | tf_op jit(solution)/shard_map/ppermute | solution.py:15
  860.9 2.0 copy-start
  868.5 401.2 %all-reduce.17.cloned.1.call-start = ((), (), s32[]{:S(2)}) async-start(), calls=%async_computation.5 | async-start | bytes 2097152 | tf_op jit(solution)/shard_map/psum | solution.py:56
  868.6 48.2 %collective-permute-start.5 = (f32[1024,256]{1,0:T(8,128)}, f32[1024,256]{1,0:T(8,128)}, u32[]{:S(2)}, u32[]{:S(2)}) collective-permute-start(f32[1024,256]{1,0:T(8,128)} %get-tuple-element.8), channel_id=1, source_target_pairs={{3,0},{0,1},{1,2},{2,3},{7,4},{4,5},{5,6},{6,7},{11,8},{8,9},{9,10... | collective-permute-start | bytes 3145736 | tf_op jit(solution)/shard_map/ppermute | solution.py:15
Sparse Core Ops, SparseCore 0:
  27.2 354.7 all-reduce.8
  385.2 43.6 all-reduce.6
  449.2 353.8 all-reduce.12
  806.2 43.8 all-reduce.10
  868.7 44.7 all-reduce.14
  915.9 353.7 all-reduce.16
where the time goes:
time: 1290 us; the launch traced here: 1280 us
  waiting for transfers between devices  1170 us (91%)
  matrix products  73.8 us (6%)
  other arithmetic  14.9 us (1%)
  between operations  14.4 us (1%)
    psum x3, waiting for transfers between devices, shards(): col_total = lax.psum(product, 'row')  1040 us
    psum x3, waiting for transfers between devices, shards(): row_total = lax.psum(row_part, 'col')  98.4 us
    ppermute x6, waiting for transfers between devices, passed_along(): return lax.ppermute(block, axis, route)  30.4 us
    dot_general x3, matrix products, swivel_residual(): jnp.dot(row_vecs, col_vecs.T, precision=highest, preferred_element_type=j...  28.7 us
    dot_general x3, matrix products, shards(): lax.dot_general(residual, row_vecs, (((0,), (0,)), ((), ())), precision=h...  26.1 us
  transfers between devices with their start and end apart: 12, of which 8 were waited for; matrix products, arithmetic and copies ran while one was open for 3% of the time, Pallas kernels for 0%

commit v1 on v0

v1 whole, which is shorter than its diff:
```python
import functools
import math

import jax
import jax.numpy as jnp
from jax import lax
from jax.experimental import pallas as pl
from jax.experimental.pallas import tpu as pltpu
from jax.sharding import Mesh, PartitionSpec as P

learn_rate = 0.5
f32 = jnp.float32
bf16 = jnp.bfloat16
tile = 256

NN = (((1,), (0,)), ((), ()))
NT = (((1,), (1,)), ((), ()))
TN = (((0,), (0,)), ((), ()))


def halves(v):
    high = v.astype(bf16)
    return high, (v - high.astype(f32)).astype(bf16)


def dot3(a, b, dims):
    def one(x, y):
        return lax.dot_general(x, y, dims, preferred_element_type=f32)

    return one(a[0], b[0]) + (one(a[0], b[1]) + one(a[1], b[0]))


def residual_kernel(
    block_ref, row_ref, colt_ref, row_bias_ref, col_bias_ref,
    product_ref, high_ref, low_ref,
    row_high, row_low, rowt_high, rowt_low, bias,
):
    rows = row_ref.shape[0]

    @pl.when(pl.program_id(0) == 0)
    def _():
        for t in range(rows // tile):
            part = pl.ds(t * tile, tile)
            high, low = halves(row_ref[part, :])
            row_high[part, :] = high
            row_low[part, :] = low
            rowt_high[:, part] = high.T
            rowt_low[:, part] = low.T
        for t in range(rows // 128):
            bias[pl.ds(t * 128, 128), :] = jnp.broadcast_to(row_bias_ref[t:t + 1, :], (128, 128)).T

    cols = halves(colt_ref[...])
    col_bias = col_bias_ref[...]
    total = None
    for t in range(rows // tile):
        part = pl.ds(t * tile, tile)
        scores = dot3((row_high[part, :], row_low[part, :]), cols, NN)
        row_bias = bias[part, :]
        shifted = scores + (jnp.concatenate([row_bias] * (tile // 128), axis=1) + col_bias)
        block = block_ref[0, part, :]
        values = jnp.maximum(block.astype(f32), 1.0)
        confidence = 0.1 + 0.25 * (values * lax.rsqrt(values))
        seen = confidence * (shifted - jnp.log(values))
        unseen = 0.5 + 0.5 * jnp.tanh(0.5 * shifted)
        high, low = halves(jnp.where(block > 0, seen, unseen))
        high_ref[part, :] = high
        low_ref[part, :] = low
        term = dot3((rowt_high[:, part], rowt_low[:, part]), (high, low), NN)
        total = term if total is None else total + term
    product_ref[...] = total


def residual_and_product(turn, counts, row_vecs, colt, row_bias, col_bias):
    _, rows, cols = counts.shape
    k = row_vecs.shape[1]
    return pl.pallas_call(
        residual_kernel,
        grid=(cols // tile,),
        in_specs=[
            pl.BlockSpec((1, rows, tile), lambda c: (turn, 0, c)),
            pl.BlockSpec((rows, k), lambda c: (0, 0)),
            pl.BlockSpec((k, tile), lambda c: (0, c)),
            pl.BlockSpec((rows // 128, 128), lambda c: (0, 0)),
            pl.BlockSpec((1, tile), lambda c: (0, c)),
        ],
        out_specs=[
            pl.BlockSpec((k, tile), lambda c: (0, c)),
            pl.BlockSpec((rows, tile), lambda c: (0, c)),
            pl.BlockSpec((rows, tile), lambda c: (0, c)),
        ],
        out_shape=[
            jax.ShapeDtypeStruct((k, cols), f32),
            jax.ShapeDtypeStruct((rows, cols), bf16),
            jax.ShapeDtypeStruct((rows, cols), bf16),
        ],
        scratch_shapes=[
            pltpu.VMEM((rows, k), bf16),
            pltpu.VMEM((rows, k), bf16),
            pltpu.VMEM((k, rows), bf16),
            pltpu.VMEM((k, rows), bf16),
            pltpu.VMEM((rows, 128), f32),
        ],
        compiler_params=pltpu.CompilerParams(vmem_limit_bytes=40 * 2**20),
        cost_estimate=pl.CostEstimate(
            flops=12 * rows * cols * k, bytes_accessed=9 * rows * cols, transcendentals=3 * rows * cols
        ),
        name="residual",
    )(counts, row_vecs, colt, row_bias, col_bias)


def row_part_kernel(high_ref, low_ref, colt_ref, out_ref, col_high, col_low):
    @pl.when(pl.program_id(0) == 0)
    def _():
        high, low = halves(colt_ref[...])
        col_high[...] = high
        col_low[...] = low

    out_ref[...] = dot3((high_ref[...], low_ref[...]), (col_high[...], col_low[...]), NT)


def row_part_of(high, low, colt):
    rows, cols = high.shape
    k = colt.shape[0]
    return pl.pallas_call(
        row_part_kernel,
        grid=(rows // tile,),
        in_specs=[
            pl.BlockSpec((tile, cols), lambda r: (r, 0)),
            pl.BlockSpec((tile, cols), lambda r: (r, 0)),
            pl.BlockSpec((k, cols), lambda r: (0, 0)),
        ],
        out_specs=pl.BlockSpec((tile, k), lambda r: (r, 0)),
        out_shape=jax.ShapeDtypeStruct((rows, k), f32),
        scratch_shapes=[pltpu.VMEM((k, cols), bf16), pltpu.VMEM((k, cols), bf16)],
        compiler_params=pltpu.CompilerParams(vmem_limit_bytes=24 * 2**20),
        cost_estimate=pl.CostEstimate(
            flops=6 * rows * cols * k, bytes_accessed=4 * rows * cols, transcendentals=0
        ),
        name="row_part",
    )(high, low, colt)


def adagrad(vecs, sums, grad):
    new_sums = sums + grad * grad
    return (vecs - learn_rate * grad / jnp.sqrt(new_sums), new_sums)


def swap(block, axis):
    n = lax.axis_size(axis)
    return lax.ppermute(block, axis, [(i, i ^ 1) for i in range(n)])


def to_next_place(block):
    chips, cores = lax.axis_size("chip"), lax.axis_size("core")
    n = chips * cores
    return lax.ppermute(block, ("chip", "core"), [(i, (i + 1) % n) for i in range(n)])


def to_next_place_and_far(block):
    chips, cores = lax.axis_size("chip"), lax.axis_size("core")
    n = chips * cores
    route = [(h * n + i, (1 - h) * n + (i + 1) % n) for h in range(2) for i in range(n)]
    return lax.ppermute(block, ("far", "chip", "core"), route)


def row_sum(part):
    core = lax.axis_index("core")
    half = part.shape[0] // 2
    two = part.reshape(2, half, part.shape[1])
    mine = lax.dynamic_index_in_dim(two, core, 0, keepdims=False)
    other = lax.dynamic_index_in_dim(two, 1 - core, 0, keepdims=False)
    mine = mine + swap(other, "core")
    mine = mine + swap(mine, "chip")
    other = swap(mine, "core")
    first = jnp.where(core == 0, mine, other)
    second = jnp.where(core == 0, other, mine)
    return jnp.concatenate([first, second], axis=0)


plane = ("x", "z")


def gathered(piece):
    n = lax.axis_size("x") * lax.axis_size("z")
    wide = jnp.broadcast_to(piece[None], (n,) + piece.shape)
    return lax.all_to_all(wide, plane, 0, 0)


def shards(counts, row_embed, row_accum, col_embed, col_accum, row_log, col_log):
    row_vecs, row_sums = (row_embed, row_accum)
    colt = col_embed.T
    colt_sums = col_accum.T
    row_bias = row_log.reshape(-1, 128)
    col_bias = col_log.reshape(1, -1)
    n_plane = lax.axis_size("x") * lax.axis_size("z")
    n_row = n_plane * lax.axis_size("far")
    n_col = lax.axis_size("chip") * lax.axis_size("core")
    row_scale = math.sqrt(n_col * col_embed.shape[0])
    col_scale = math.sqrt(n_row * row_embed.shape[0])
    k, cols = colt.shape
    size = k // n_plane
    me = lax.axis_index("x") * lax.axis_size("z") + lax.axis_index("z")
    piece = lax.dynamic_slice_in_dim(colt, me * size, size, 0)
    piece_sums = lax.dynamic_slice_in_dim(colt_sums, me * size, size, 0)
    turns = counts.shape[0]
    for turn in range(turns):
        product, high, low = residual_and_product(turn, counts, row_vecs, colt, row_bias, col_bias)
        terms = lax.all_to_all(product.reshape(n_plane, size, cols), plane, 0, 0)
        row_total = row_sum(row_part_of(high, low, colt))
        total = jnp.sum(terms, axis=0)
        if turn < turns - 1:
            piece, piece_sums, col_bias = to_next_place((piece, piece_sums, col_bias))
            total = to_next_place(total) + to_next_place_and_far(total)
        else:
            total = total + swap(total, "far")
        piece, piece_sums = adagrad(piece, piece_sums, total / col_scale)
        if turn < turns - 1:
            colt = gathered(piece).reshape(k, cols)
        row_vecs, row_sums = adagrad(row_vecs, row_sums, row_total / row_scale)
    both = gathered(jnp.stack([piece, piece_sums]))
    return (row_vecs, row_sums, both[:, 0].reshape(k, cols).T, both[:, 1].reshape(k, cols).T)


def solution(mesh):
    fine = Mesh(mesh.devices.reshape(4, 4, 2, 2, 2), ("x", "z", "far", "chip", "core"))
    row = ("x", "z", "far")
    col = ("chip", "core")
    return jax.shard_map(
        shards,
        mesh=fine,
        in_specs=(
            P(None, row, col),
            P(row, None),
            P(row, None),
            P(col, None),
            P(col, None),
            P(row),
            P(col),
        ),
        out_specs=(P(row, None), P(row, None), P(col, None), P(col, None)),
        check_vma=False,
    )
```

time: 1290 us -> 214 us (0.17)
  waiting for transfers between devices: 1170 us -> 105 us
  matrix products: 73.8 us -> 0 us
  starting transfers between devices: 2.44 us -> 38.5 us
  Pallas kernels: 0 us -> 33 us
  local copies, waits for them, and re-layouts: 5.86 us -> 21.1 us
  between operations: 14.4 us -> 1.19 us
    psum x6 -> x0, waiting for transfers between devices: 1140 us -> none  [the longest x3 1040 us: shards(): col_total = lax.psum(product, 'row')]
    all_to_all x0 -> x6, waiting for transfers between devices: none -> 82.7 us  [the longest x3 43.5 us: gathered(): return lax.all_to_all(wide, plane, 0, 0)]
    dot_general x9 -> x0, matrix products: 73.8 us -> none  [the longest x3 28.7 us: swivel_residual(): jnp.dot(row_vecs, col_vecs.T, precision=highest, preferred_element_type=j...]
    pallas_call x0 -> x6, Pallas kernels: none -> 33 us  [the longest x3 25.1 us: residual_and_product(): pl.pallas_call(residual_kernel, grid=(cols // tile,), in_specs=[pl.BlockS...]
    all_to_all x0 -> x6, starting transfers between devices: none -> 27.7 us  [the longest x3 15.9 us: shards(): terms = lax.all_to_all(product.reshape(n_plane, size, cols), plane, 0, 0)]
    ppermute x6 -> x20, waiting for transfers between devices: 30.4 us -> 22.2 us  [the longest x10 18 us: swap(): return lax.ppermute(block, axis, [(i, i ^ 1) for i in range(n)])]
  transfers between devices with their start and end apart: 12 -> 26, of which waited for: 8 -> 14; matrix products, arithmetic and copies ran while one was open for 3% -> 9% of each run, Pallas kernels for 0% -> 1%
where the time goes in v1:
time: 214 us; the launch traced here: 213 us
  waiting for transfers between devices  105 us (49%)
  starting transfers between devices  38.5 us (18%)
  Pallas kernels  33 us (15%)
  local copies, waits for them, and re-layouts  21.1 us (10%)
  other arithmetic  14.1 us (7%)
    all_to_all x3, waiting for transfers between devices, gathered(): return lax.all_to_all(wide, plane, 0, 0)  43.5 us
    all_to_all x3, waiting for transfers between devices, shards(): terms = lax.all_to_all(product.reshape(n_plane, size, cols), plane, 0, 0)  39.2 us
    pallas_call x3, Pallas kernels, residual_and_product(): pl.pallas_call(residual_kernel, grid=(cols // tile,), in_specs=[pl.BlockS...  25.1 us
    ppermute x10, waiting for transfers between devices, swap(): return lax.ppermute(block, axis, [(i, i ^ 1) for i in range(n)])  18 us
    all_to_all x3, starting transfers between devices, shards(): terms = lax.all_to_all(product.reshape(n_plane, size, cols), plane, 0, 0)  15.9 us
    unnamed x52, local copies, waits for them, and re-layouts  12.9 us
    all_to_all x3, starting transfers between devices, gathered(): return lax.all_to_all(wide, plane, 0, 0)  11.8 us
    pallas_call x3, Pallas kernels, row_part_of(): pl.pallas_call(row_part_kernel, grid=(rows // tile,), in_specs=[pl.BlockS...  7.88 us
  transfers between devices with their start and end apart: 26, of which 14 were waited for; matrix products, arithmetic and copies ran while one was open for 9% of the time, Pallas kernels for 1%

profile of v1, /device:TPU:8, one launch (start us, length us, event | category | flops | bytes accessed | tf_op | source)
XLA Modules:
  0.0 212.8 jit_solution(14972569957327906440)
XLA Ops:
  2.4 8.3 %residual.3 = (f32[256,1024]{1,0:T(8,128)S(1)}, bf16[1024,1024]{1,0:T(8,128)(2,1)S(1)}, bf16[1024,1024]{1,0:T(8,128)(2,1)S(1)}) custom-call(s32[3,1024,1024]{2,1,0:T(8,128)} %block_ref.5, f32[1024,256]{1,0:T(8,128)S(1)} %copy-done.2, f32[256,1024]{1,0:T(8,128)S(1)} %bitcast.40, f32[8,128]{1,0:T(8,128)S(1)} %bitcast.54, f32[1,1024]{1,0:T(1,128)S(1)} %bitcast.57), custom_call_target="tpu_custom_call" | custom-call | flops 3221225472 | bytes 9437184 | tf_op jit(solution)/shard_map/residual/pallas_call | solution.py:76
  10.7 2.6 %row_part.3 = f32[1024,256]{1,0:T(8,128)S(1)} custom-call(bf16[1024,1024]{1,0:T(8,128)(2,1)S(1)} %get-tuple-element.13.high_ref, bf16[1024,1024]{1,0:T(8,128)(2,1)S(1)} %get-tuple-element.14.low_ref, f32[256,1024]{1,0:T(8,128)S(1)} %bitcast.41), custom_call_target="tpu_custom_call" | custom-call | flops 1610612736 | bytes 4194304 | tf_op jit(solution)/shard_map/row_part/pallas_call | solution.py:124
  15.2 7.9 %all-to-all-start = ((f32[16,16,1024]{2,1,0:T(8,128)}), f32[16,16,1024]{2,1,0:T(8,128)}, u32[]{:S(2)}, u32[]{:S(2)}) async-start(f32[16,16,1024]{2,1,0:T(8,128)} %bitcast.52), calls=%async_computation | async-start | bytes 2097152 | tf_op jit(solution)/shard_map/all_to_all | solution.py:208
  23.1 2.1 bitcast_add_fusion.2
  29.6 12.1 %all-to-all-done = f32[16,16,1024]{2,1,0:T(8,128)} async-done(((f32[16,16,1024]{2,1,0:T(8,128)}), f32[16,16,1024]{2,1,0:T(8,128)}, u32[]{:S(2)}, u32[]{:S(2)}) %all-to-all-start) | async-done | bytes 1048608 | tf_op jit(solution)/shard_map/all_to_all | solution.py:208
  49.8 3.7 %all-to-all-start.1 = ((f32[16,16,1024]{2,1,0:T(8,128)}), f32[16,16,1024]{2,1,0:T(8,128)S(1)}, u32[]{:S(2)}, u32[]{:S(2)}) async-start(f32[16,16,1024]{2,1,0:T(8,128)} %broadcast_in_dim.6), calls=%async_computation.1 | async-start | bytes 2097152 | tf_op jit(solution)/shard_map/all_to_all | solution.py:186
  53.8 1.8 multiply_subtract_fusion.2.row_ref
  56.7 14.6 %all-to-all-done.1 = f32[16,16,1024]{2,1,0:T(8,128)S(1)} async-done(((f32[16,16,1024]{2,1,0:T(8,128)}), f32[16,16,1024]{2,1,0:T(8,128)S(1)}, u32[]{:S(2)}, u32[]{:S(2)}) %all-to-all-start.1) | async-done | bytes 1048608 | tf_op jit(solution)/shard_map/all_to_all | solution.py:186
  71.3 8.3 %residual.4 = (f32[256,1024]{1,0:T(8,128)S(1)}, bf16[1024,1024]{1,0:T(8,128)(2,1)S(1)}, bf16[1024,1024]{1,0:T(8,128)(2,1)S(1)}) custom-call(s32[3,1024,1024]{2,1,0:T(8,128)} %block_ref.5, f32[1024,256]{1,0:T(8,128)S(1)} %multiply_subtract_fusion.2.row_ref, f32[256,1024]{1,0:T(8,128)S(1)} %bitcast.44, f32[8,128]{1,0:T(8,128)S(1)} %bitcast.55, ...), custom_call_target="tpu_custom_call" | custom-call | flops 3221225472 | bytes 9437184 | tf_op jit(solution)/shard_map/residual/pallas_call | solution.py:76
  79.6 2.6 %row_part.4 = f32[1024,256]{1,0:T(8,128)S(1)} custom-call(bf16[1024,1024]{1,0:T(8,128)(2,1)S(1)} %get-tuple-element.16.high_ref, bf16[1024,1024]{1,0:T(8,128)(2,1)S(1)} %get-tuple-element.17.low_ref, f32[256,1024]{1,0:T(8,128)S(1)} %bitcast.45), custom_call_target="tpu_custom_call" | custom-call | flops 1610612736 | bytes 4194304 | tf_op jit(solution)/shard_map/row_part/pallas_call | solution.py:124
  83.1 3.7 %all-to-all-start.2 = ((f32[16,16,1024]{2,1,0:T(8,128)}), f32[16,16,1024]{2,1,0:T(8,128)S(1)}, u32[]{:S(2)}, u32[]{:S(2)}) async-start(f32[16,16,1024]{2,1,0:T(8,128)} %bitcast.53), calls=%async_computation.2 | async-start | bytes 2097152 | tf_op jit(solution)/shard_map/all_to_all | solution.py:208
  86.7 1.9 bitcast_add_fusion.1
  90.8 14.9 %all-to-all-done.2 = f32[16,16,1024]{2,1,0:T(8,128)S(1)} async-done(((f32[16,16,1024]{2,1,0:T(8,128)}), f32[16,16,1024]{2,1,0:T(8,128)S(1)}, u32[]{:S(2)}, u32[]{:S(2)}) %all-to-all-start.2) | async-done | bytes 1048608 | tf_op jit(solution)/shard_map/all_to_all | solution.py:208
  111.2 3.7 %all-to-all-start.3 = ((f32[16,16,1024]{2,1,0:T(8,128)}), f32[16,16,1024]{2,1,0:T(8,128)S(1)}, u32[]{:S(2)}, u32[]{:S(2)}) async-start(f32[16,16,1024]{2,1,0:T(8,128)} %broadcast_in_dim.7), calls=%async_computation.3 | async-start | bytes 2097152 | tf_op jit(solution)/shard_map/all_to_all | solution.py:186
  118.0 16.4 %all-to-all-done.3 = f32[16,16,1024]{2,1,0:T(8,128)S(1)} async-done(((f32[16,16,1024]{2,1,0:T(8,128)}), f32[16,16,1024]{2,1,0:T(8,128)S(1)}, u32[]{:S(2)}, u32[]{:S(2)}) %all-to-all-start.3) | async-done | bytes 1048608 | tf_op jit(solution)/shard_map/all_to_all | solution.py:186
  134.4 8.6 %residual.5 = (f32[256,1024]{1,0:T(8,128)}, bf16[1024,1024]{1,0:T(8,128)(2,1)S(1)}, bf16[1024,1024]{1,0:T(8,128)(2,1)S(1)}) custom-call(s32[3,1024,1024]{2,1,0:T(8,128)} %block_ref.5, f32[1024,256]{1,0:T(8,128)S(1)} %multiply_subtract_fusion.1.row_ref, f32[256,1024]{1,0:T(8,128)S(1)} %bitcast.42, f32[8,128]{1,0:T(8,128)S(1)} %bitcast.56, ...), custom_call_target="tpu_custom_call" | custom-call | flops 3221225472 | bytes 9437184 | tf_op jit(solution)/shard_map/residual/pallas_call | solution.py:76
  145.7 4.3 %all-to-all-start.4 = ((f32[16,16,1024]{2,1,0:T(8,128)}), f32[16,16,1024]{2,1,0:T(8,128)}, u32[]{:S(2)}, u32[]{:S(2)}) async-start(f32[16,16,1024]{2,1,0:T(8,128)} %bitcast.18), calls=%async_computation.4 | async-start | bytes 2097152 | tf_op jit(solution)/shard_map/all_to_all | solution.py:208
  153.2 2.6 %row_part.5 = f32[1024,256]{1,0:T(8,128)S(1)} custom-call(bf16[1024,1024]{1,0:T(8,128)(2,1)S(1)} %copy-done.5, bf16[1024,1024]{1,0:T(8,128)(2,1)S(1)} %copy-done.7, f32[256,1024]{1,0:T(8,128)S(1)} %bitcast.43), custom_call_target="tpu_custom_call" | custom-call | flops 1610612736 | bytes 4194304 | tf_op jit(solution)/shard_map/row_part/pallas_call | solution.py:124
  155.9 12.2 %all-to-all-done.4 = f32[16,16,1024]{2,1,0:T(8,128)} async-done(((f32[16,16,1024]{2,1,0:T(8,128)}), f32[16,16,1024]{2,1,0:T(8,128)}, u32[]{:S(2)}, u32[]{:S(2)}) %all-to-all-start.4) | async-done | bytes 1048608 | tf_op jit(solution)/shard_map/all_to_all | solution.py:208
  169.6 5.8 %collective-permute-done.19 = f32[16,1024]{1,0:T(8,128)S(1)} collective-permute-done((f32[16,1024]{1,0:T(8,128)S(1)}, f32[16,1024]{1,0:T(8,128)S(1)}, u32[]{:S(2)}, u32[]{:S(2)}) %collective-permute-start.19) | collective-permute-done | bytes 65568 | tf_op jit(solution)/shard_map/ppermute | solution.py:150
  177.0 4.4 %all-to-all-start.5 = ((f32[16,2,16,1024]{3,2,1,0:T(8,128)}), f32[16,2,16,1024]{3,2,1,0:T(8,128)}, u32[]{:S(2)}, u32[]{:S(2)}) async-start(f32[16,2,16,1024]{3,2,1,0:T(8,128)} %broadcast_in_dim.8), calls=%async_computation.5 | async-start | bytes 4194304 | tf_op jit(solution)/shard_map/all_to_all | solution.py:186
  181.7 10.4 %collective-permute-done.17 = f32[512,256]{1,0:T(8,128)S(1)} collective-permute-done((f32[512,256]{1,0:T(8,128)S(1)}, f32[512,256]{1,0:T(8,128)S(1)}, u32[]{:S(2)}, u32[]{:S(2)}) %collective-permute-start.17) | collective-permute-done | bytes 524320 | tf_op jit(solution)/shard_map/ppermute | solution.py:150
  192.2 1.9 collective-permute-done.18
  196.0 12.5 %all-to-all-done.5 = f32[16,2,16,1024]{3,2,1,0:T(8,128)} async-done(((f32[16,2,16,1024]{3,2,1,0:T(8,128)}), f32[16,2,16,1024]{3,2,1,0:T(8,128)}, u32[]{:S(2)}, u32[]{:S(2)}) %all-to-all-start.5) | async-done | bytes 2097184 | tf_op jit(solution)/shard_map/all_to_all | solution.py:186
  (114 shorter events, 44.4 us)
Async XLA Ops:
  15.2 7.9 %collective-permute-start = (f32[512,256]{1,0:T(8,128)}, f32[512,256]{1,0:T(8,128)}, u32[]{:S(2)}, u32[]{:S(2)}) collective-permute-start(f32[512,256]{1,0:T(8,128)} %dynamic-slice_bitcast_fusion.2), channel_id=1, source_target_pairs={{0,1},{1,0},{2,3},{3,2},{4,5},{5,4},{6,7},{7,6},{8,9},{9,8},{10,11... | collective-permute-start | bytes 1572872 | tf_op jit(solution)/shard_map/ppermute | solution.py:150
  15.2 26.5 %all-to-all-start = ((f32[16,16,1024]{2,1,0:T(8,128)}), f32[16,16,1024]{2,1,0:T(8,128)}, u32[]{:S(2)}, u32[]{:S(2)}) async-start(f32[16,16,1024]{2,1,0:T(8,128)} %bitcast.52), calls=%async_computation | async-start | bytes 2097152 | tf_op jit(solution)/shard_map/all_to_all | solution.py:208
  25.2 19.5 %collective-permute-start.1 = (f32[512,256]{1,0:T(8,128)}, f32[512,256]{1,0:T(8,128)}, u32[]{:S(2)}, u32[]{:S(2)}) collective-permute-start(f32[512,256]{1,0:T(8,128)} %bitcast_add_fusion.2), channel_id=1, source_target_pairs={{0,2},{2,0},{1,3},{3,1},{4,6},{6,4},{5,7},{7,5},{8,10},{10,8},{9,1... | collective-permute-start | bytes 1572872 | tf_op jit(solution)/shard_map/ppermute | solution.py:150
  27.8 18.6 %collective-permute-start.6 = (f32[16,1024]{1,0:T(8,128)S(1)}, f32[16,1024]{1,0:T(8,128)S(1)}, u32[]{:S(2)}, u32[]{:S(2)}) collective-permute-start(f32[16,1024]{1,0:T(8,128)S(1)} %bitcast.61), channel_id=1, source_target_pairs={{0,1},{1,2},{2,3},{3,0},{4,5},{5,6},{6,7},{7,4},{8,9},{9,10},{10,1... | collective-permute-start | bytes 196616 | tf_op jit(solution)/shard_map/ppermute | solution.py:156
  27.9 18.5 %collective-permute-start.3 = (f32[16,1024]{1,0:T(8,128)S(1)}, f32[16,1024]{1,0:T(8,128)S(1)}, u32[]{:S(2)}, u32[]{:S(2)}) collective-permute-start(f32[16,1024]{1,0:T(8,128)S(1)} %dynamic-slice_bitcast_fusion.3), channel_id=1, source_target_pairs={{0,1},{1,2},{2,3},{3,0},{4,5},{5,6},{6,7},{7,4},{8,9},{9,10},{10,1... | collective-permute-start | bytes 196616 | tf_op jit(solution)/shard_map/ppermute | solution.py:156
  42.9 3.8 %collective-permute-start.5 = (f32[16,1024]{1,0:T(8,128)S(1)}, f32[16,1024]{1,0:T(8,128)S(1)}, u32[]{:S(2)}, u32[]{:S(2)}) collective-permute-start(f32[16,1024]{1,0:T(8,128)S(1)} %reduce_sum.27), channel_id=1, source_target_pairs={{0,5},{1,6},{2,7},{3,4},{4,1},{5,2},{6,3},{7,0},{8,13},{9,14},{10,... | collective-permute-start | bytes 196616 | tf_op jit(solution)/shard_map/ppermute | solution.py:163
  43.6 4.5 %collective-permute-start.4 = (f32[16,1024]{1,0:T(8,128)S(1)}, f32[16,1024]{1,0:T(8,128)S(1)}, u32[]{:S(2)}, u32[]{:S(2)}) collective-permute-start(f32[16,1024]{1,0:T(8,128)S(1)} %reduce_sum.27), channel_id=1, source_target_pairs={{0,1},{1,2},{2,3},{3,0},{4,5},{5,6},{6,7},{7,4},{8,9},{9,10},{10,1... | collective-permute-start | bytes 196616 | tf_op jit(solution)/shard_map/ppermute | solution.py:156
  45.9 7.7 %collective-permute-start.2 = (f32[512,256]{1,0:T(8,128)S(1)}, f32[512,256]{1,0:T(8,128)S(1)}, u32[]{:S(2)}, u32[]{:S(2)}) collective-permute-start(f32[512,256]{1,0:T(8,128)S(1)} %add.67), channel_id=1, source_target_pairs={{0,1},{1,0},{2,3},{3,2},{4,5},{5,4},{6,7},{7,6},{8,9},{9,8},{10,11... | collective-permute-start | bytes 1572872 | tf_op jit(solution)/shard_map/ppermute | solution.py:150
  49.8 21.4 %all-to-all-start.1 = ((f32[16,16,1024]{2,1,0:T(8,128)}), f32[16,16,1024]{2,1,0:T(8,128)S(1)}, u32[]{:S(2)}, u32[]{:S(2)}) async-start(f32[16,16,1024]{2,1,0:T(8,128)} %broadcast_in_dim.6), calls=%async_computation.1 | async-start | bytes 2097152 | tf_op jit(solution)/shard_map/all_to_all | solution.py:186
  83.0 3.7 %collective-permute-start.8 = (f32[512,256]{1,0:T(8,128)}, f32[512,256]{1,0:T(8,128)}, u32[]{:S(2)}, u32[]{:S(2)}) collective-permute-start(f32[512,256]{1,0:T(8,128)} %dynamic-slice_bitcast_fusion.1), channel_id=1, source_target_pairs={{0,1},{1,0},{2,3},{3,2},{4,5},{5,4},{6,7},{7,6},{8,9},{9,8},{10,11... | collective-permute-start | bytes 1572872 | tf_op jit(solution)/shard_map/ppermute | solution.py:150
  83.1 22.6 %all-to-all-start.2 = ((f32[16,16,1024]{2,1,0:T(8,128)}), f32[16,16,1024]{2,1,0:T(8,128)S(1)}, u32[]{:S(2)}, u32[]{:S(2)}) async-start(f32[16,16,1024]{2,1,0:T(8,128)} %bitcast.53), calls=%async_computation.2 | async-start | bytes 2097152 | tf_op jit(solution)/shard_map/all_to_all | solution.py:208
  88.6 18.4 %collective-permute-start.9 = (f32[512,256]{1,0:T(8,128)}, f32[512,256]{1,0:T(8,128)S(1)}, u32[]{:S(2)}, u32[]{:S(2)}) collective-permute-start(f32[512,256]{1,0:T(8,128)} %bitcast_add_fusion.1), channel_id=1, source_target_pairs={{0,2},{2,0},{1,3},{3,1},{4,6},{6,4},{5,7},{7,5},{8,10},{10,8},{9,1... | collective-permute-start | bytes 1572872 | tf_op jit(solution)/shard_map/ppermute | solution.py:150
  89.7 19.7 %collective-permute-start.11 = (f32[16,1024]{1,0:T(8,128)S(1)}, f32[16,1024]{1,0:T(8,128)S(1)}, u32[]{:S(2)}, u32[]{:S(2)}) collective-permute-start(f32[16,1024]{1,0:T(8,128)S(1)} %get-tuple-element.43), channel_id=1, source_target_pairs={{0,1},{1,2},{2,3},{3,0},{4,5},{5,6},{6,7},{7,4},{8,9},{9,10},{10,1... | collective-permute-start | bytes 196616 | tf_op jit(solution)/shard_map/ppermute | solution.py:156
  90.0 19.5 %collective-permute-start.14 = (f32[16,1024]{1,0:T(8,128)}, f32[16,1024]{1,0:T(8,128)S(1)}, u32[]{:S(2)}, u32[]{:S(2)}) collective-permute-start(f32[16,1024]{1,0:T(8,128)} %get-tuple-element.42), channel_id=1, source_target_pairs={{0,1},{1,2},{2,3},{3,0},{4,5},{5,6},{6,7},{7,4},{8,9},{9,10},{10,1... | collective-permute-start | bytes 196616 | tf_op jit(solution)/shard_map/ppermute | solution.py:156
  105.7 3.8 %collective-permute-start.13 = (f32[16,1024]{1,0:T(8,128)S(1)}, f32[16,1024]{1,0:T(8,128)S(1)}, u32[]{:S(2)}, u32[]{:S(2)}) collective-permute-start(f32[16,1024]{1,0:T(8,128)S(1)} %reduce_sum.28), channel_id=1, source_target_pairs={{0,5},{1,6},{2,7},{3,4},{4,1},{5,2},{6,3},{7,0},{8,13},{9,14},{10,... | collective-permute-start | bytes 196616 | tf_op jit(solution)/shard_map/ppermute | solution.py:163
  105.9 4.1 %collective-permute-start.12 = (f32[16,1024]{1,0:T(8,128)S(1)}, f32[16,1024]{1,0:T(8,128)S(1)}, u32[]{:S(2)}, u32[]{:S(2)}) collective-permute-start(f32[16,1024]{1,0:T(8,128)S(1)} %reduce_sum.28), channel_id=1, source_target_pairs={{0,1},{1,2},{2,3},{3,0},{4,5},{5,6},{6,7},{7,4},{8,9},{9,10},{10,1... | collective-permute-start | bytes 196616 | tf_op jit(solution)/shard_map/ppermute | solution.py:156
  108.1 7.9 %collective-permute-start.10 = (f32[512,256]{1,0:T(8,128)S(1)}, f32[512,256]{1,0:T(8,128)S(1)}, u32[]{:S(2)}, u32[]{:S(2)}) collective-permute-start(f32[512,256]{1,0:T(8,128)S(1)} %add.74), channel_id=1, source_target_pairs={{0,1},{1,0},{2,3},{3,2},{4,5},{5,4},{6,7},{7,6},{8,9},{9,8},{10,11... | collective-permute-start | bytes 1572872 | tf_op jit(solution)/shard_map/ppermute | solution.py:150
  111.2 23.2 %all-to-all-start.3 = ((f32[16,16,1024]{2,1,0:T(8,128)}), f32[16,16,1024]{2,1,0:T(8,128)S(1)}, u32[]{:S(2)}, u32[]{:S(2)}) async-start(f32[16,16,1024]{2,1,0:T(8,128)} %broadcast_in_dim.7), calls=%async_computation.3 | async-start | bytes 2097152 | tf_op jit(solution)/shard_map/all_to_all | solution.py:186
  114.9 3.1 %collective-permute-start.15 = (f32[1,1024]{1,0:T(1,128)S(1)}, f32[1,1024]{1,0:T(1,128)S(1)}, u32[]{:S(2)}, u32[]{:S(2)}) collective-permute-start(f32[1,1024]{1,0:T(1,128)S(1)} %collective-permute-done.7.col_bias_ref), channel_id=1, source_target_pairs={{0,1},{1,2},{2,3},{3,0},{4,5},{5,6},{6,7},{7,4},{8,9},{9,10},{10,1... | collective-permute-start | bytes 12296 | tf_op jit(solution)/shard_map/ppermute | solution.py:156
  145.7 22.5 %all-to-all-start.4 = ((f32[16,16,1024]{2,1,0:T(8,128)}), f32[16,16,1024]{2,1,0:T(8,128)}, u32[]{:S(2)}, u32[]{:S(2)}) async-start(f32[16,16,1024]{2,1,0:T(8,128)} %bitcast.18), calls=%async_computation.4 | async-start | bytes 2097152 | tf_op jit(solution)/shard_map/all_to_all | solution.py:208
  155.9 25.6 %collective-permute-start.16 = (f32[512,256]{1,0:T(8,128)S(1)}, f32[512,256]{1,0:T(8,128)S(1)}, u32[]{:S(2)}, u32[]{:S(2)}) collective-permute-start(f32[512,256]{1,0:T(8,128)S(1)} %dynamic-slice_bitcast_fusion), channel_id=1, source_target_pairs={{0,1},{1,0},{2,3},{3,2},{4,5},{5,4},{6,7},{7,6},{8,9},{9,8},{10,11... | collective-permute-start | bytes 1572872 | tf_op jit(solution)/shard_map/ppermute | solution.py:150
  169.5 5.8 %collective-permute-start.19 = (f32[16,1024]{1,0:T(8,128)S(1)}, f32[16,1024]{1,0:T(8,128)S(1)}, u32[]{:S(2)}, u32[]{:S(2)}) collective-permute-start(f32[16,1024]{1,0:T(8,128)S(1)} %reduce_sum.29), channel_id=1, source_target_pairs={{0,4},{4,0},{1,5},{5,1},{2,6},{6,2},{3,7},{7,3},{8,12},{12,8},{9,1... | collective-permute-start | bytes 196616 | tf_op jit(solution)/shard_map/ppermute | solution.py:150
  177.0 31.5 %all-to-all-start.5 = ((f32[16,2,16,1024]{3,2,1,0:T(8,128)}), f32[16,2,16,1024]{3,2,1,0:T(8,128)}, u32[]{:S(2)}, u32[]{:S(2)}) async-start(f32[16,2,16,1024]{3,2,1,0:T(8,128)} %broadcast_in_dim.8), calls=%async_computation.5 | async-start | bytes 4194304 | tf_op jit(solution)/shard_map/all_to_all | solution.py:186
  181.6 10.4 %collective-permute-start.17 = (f32[512,256]{1,0:T(8,128)S(1)}, f32[512,256]{1,0:T(8,128)S(1)}, u32[]{:S(2)}, u32[]{:S(2)}) collective-permute-start(f32[512,256]{1,0:T(8,128)S(1)} %bitcast_add_fusion), channel_id=1, source_target_pairs={{0,2},{2,0},{1,3},{3,1},{4,6},{6,4},{5,7},{7,5},{8,10},{10,8},{9,1... | collective-permute-start | bytes 1572872 | tf_op jit(solution)/shard_map/ppermute | solution.py:150
  (26 other events, 122.9 us)

commit v2 on v0

v2 whole, which is shorter than its diff:
```python
import functools
import math

import jax
import jax.numpy as jnp
from jax import lax
from jax.experimental import pallas as pl
from jax.experimental.pallas import tpu as pltpu
from jax.sharding import Mesh, PartitionSpec as P

learn_rate = 0.5
f32 = jnp.float32
bf16 = jnp.bfloat16
tile = 256
vmem_limit = 50 * 2**20
vmem_most = 50 * 2**20
vmem_small = 8 * 2**20
cross = 1

NN = (((1,), (0,)), ((), ()))
NT = (((1,), (1,)), ((), ()))
TN = (((0,), (0,)), ((), ()))


def parts(v, n):
    out = []
    for _ in range(n - 1):
        out.append(v.astype(bf16))
        v = v - out[-1].astype(f32)
    return out + [v.astype(bf16)]


def dot(a, b, dims):
    return lax.dot_general(a, b, dims, preferred_element_type=f32)


def folded(v, n):
    size = v.shape[0] // n
    total = v[(n - 1) * size:]
    for t in reversed(range(n - 1)):
        total = total + v[t * size:(t + 1) * size]
    return total


def residual_kernel(
    first, turn, counts_ref, row_in, col_in, row_bias_in, state_in,
    product_out, residual_out,
    row_ref, col_ref, row_bias_ref, col_bias_ref, product_ref,
    row_parts, rowt_parts, bias, scores, block_ref, residual_ref, sems, block_sems, residual_sems,
):
    rows, k = row_ref.shape
    cols = col_bias_ref.shape[1]
    loads = [
        pltpu.make_async_copy(source, target, sems.at[n])
        for n, (source, target) in enumerate(
            ((row_in, row_ref), (col_in, col_ref), (row_bias_in, row_bias_ref), (state_in.at[pl.ds(state_in.shape[0] - 8, 8)], col_bias_ref))
        )
    ]
    for load in loads:
        load.start()
    spans = [pl.ds(t * tile, tile) for t in range(rows // tile)]
    fetches = [
        pltpu.make_async_copy(counts_ref.at[turn, span, :], block_ref.at[span, :], block_sems.at[t])
        for t, span in enumerate(spans)
    ]
    stores = [
        pltpu.make_async_copy(residual_ref.at[span, :], residual_out.at[span, :], residual_sems.at[t])
        for t, span in enumerate(spans)
    ]
    for fetch in fetches:
        fetch.start()
    loads[0].wait()
    for t, span in enumerate(spans):
        for n, v in enumerate(parts(row_ref[span, :], 3)):
            if n < 2:
                row_parts[pl.ds(n * rows + t * tile, tile), :] = v
            rowt_parts[pl.ds(n * k, k), span] = v.T
    loads[2].wait()
    for t in range(rows // 128):
        bias[pl.ds(t * 128, 128), :] = jnp.broadcast_to(row_bias_ref[t:t + 1, :], (128, 128)).T
    loads[1].wait()
    loads[3].wait()
    col_high, col_low = parts(col_ref[...], 2)
    dims = NT if first else NN
    scores[...] = folded(dot(row_parts[...], col_high, dims), 2) + dot(row_parts[:rows, :], col_low, dims)
    col_bias = col_bias_ref[:1, :]
    total = None
    for t, span in enumerate(spans):
        row_bias = jnp.concatenate([bias[span, :]] * (cols // 128), axis=1)
        shifted = scores[span, :] + (row_bias + col_bias)
        fetches[t].wait()
        block = block_ref[span, :]
        values = jnp.maximum(block.astype(f32), 1.0)
        confidence = 0.1 + 0.25 * (values * lax.rsqrt(values))
        seen = confidence * (shifted - jnp.log(values))
        unseen = 0.5 + 0.5 * jnp.tanh(0.5 * shifted)
        residual = jnp.where(block > 0, seen, unseen)
        residual_ref[span, :] = residual
        stores[t].start()
        high, low = parts(residual, 2)
        term = folded(dot(rowt_parts[:cross * k, span], low, NN), cross)
        term = term + folded(dot(rowt_parts[:, span], high, NN), 3)
        total = term if total is None else total + term
    product_ref[...] = total
    out = pltpu.make_async_copy(product_ref, product_out, sems.at[0])
    out.start()
    for store in stores:
        store.wait()
    out.wait()


def residual_and_product(first, turn, counts, row_vecs, col_vecs, row_bias, state):
    _, rows, cols = counts.shape
    k = row_vecs.shape[1]
    steps = rows // tile
    far = pl.BlockSpec(memory_space=pltpu.HBM)
    return pl.pallas_call(
        functools.partial(residual_kernel, first, turn),
        in_specs=[far] * 5,
        out_specs=[far] * 2,
        out_shape=[
            jax.ShapeDtypeStruct((k, cols), f32),
            jax.ShapeDtypeStruct((rows, cols), f32),
        ],
        scratch_shapes=[
            pltpu.VMEM((rows, k), f32),
            pltpu.VMEM(col_vecs.shape, f32),
            pltpu.VMEM(row_bias.shape, f32),
            pltpu.VMEM((8, cols), f32),
            pltpu.VMEM((k, cols), f32),
            pltpu.VMEM((2 * rows, k), bf16),
            pltpu.VMEM((3 * k, rows), bf16),
            pltpu.VMEM((rows, 128), f32),
            pltpu.VMEM((rows, cols), f32),
            pltpu.VMEM((rows, cols), jnp.int32),
            pltpu.VMEM((rows, cols), f32),
            pltpu.SemaphoreType.DMA((4,)),
            pltpu.SemaphoreType.DMA((steps,)),
            pltpu.SemaphoreType.DMA((steps,)),
        ],
        compiler_params=pltpu.CompilerParams(vmem_limit_bytes=vmem_most),
        cost_estimate=pl.CostEstimate(flops=0, bytes_accessed=0, transcendentals=0),
        name="residual",
    )(counts, row_vecs, col_vecs, row_bias, state)


def row_part_kernel(first, half_ref, residual_ref, col_ref, out_ref, col_parts):
    @pl.when(pl.program_id(0) == 0)
    def _():
        for n, v in enumerate(parts(col_ref[...], 3)):
            col_parts[n] = v

    dims = NN if first else NT
    high, low = parts(residual_ref[...], 2)
    total = dot(high, col_parts[2], dims)
    for n in reversed(range(cross)):
        total = total + dot(low, col_parts[n], dims)
    for n in (1, 0):
        total = total + dot(high, col_parts[n], dims)
    out_ref[...] = total


def row_part_of(first, half, residual, col_vecs):
    rows, cols = residual.shape
    k = col_vecs.size // cols
    steps = rows // 2 // tile
    return pl.pallas_call(
        functools.partial(row_part_kernel, first),
        grid_spec=pltpu.PrefetchScalarGridSpec(
            num_scalar_prefetch=1,
            grid=(steps,),
            in_specs=[
                pl.BlockSpec((tile, cols), lambda r, half: (half[0] * steps + r, 0)),
                pl.BlockSpec(col_vecs.shape, lambda r, half: (0, 0)),
            ],
            out_specs=pl.BlockSpec((tile, k), lambda r, half: (r, 0)),
            scratch_shapes=[pltpu.VMEM((3,) + col_vecs.shape, bf16)],
        ),
        out_shape=jax.ShapeDtypeStruct((rows // 2, k), f32),
        compiler_params=pltpu.CompilerParams(vmem_limit_bytes=vmem_limit),
        cost_estimate=pl.CostEstimate(flops=0, bytes_accessed=0, transcendentals=0),
        name="row_part",
    )(jnp.full((1,), half, jnp.int32), residual, col_vecs)


def adagrad(vecs, sums, grad):
    new_sums = sums + grad * grad
    return (vecs - learn_rate * grad / jnp.sqrt(new_sums), new_sums)


def swap(block, axis):
    n = lax.axis_size(axis)
    return lax.ppermute(block, axis, [(i, i ^ 1) for i in range(n)])


def to_next_place(block):
    chips, cores = lax.axis_size("chip"), lax.axis_size("core")
    n = chips * cores
    return lax.ppermute(block, ("chip", "core"), [(i, (i + 1) % n) for i in range(n)])


def to_next_place_and_far(block):
    chips, cores = lax.axis_size("chip"), lax.axis_size("core")
    n = chips * cores
    route = [(h * n + i, (1 - h) * n + (i + 1) % n) for h in range(2) for i in range(n)]
    return lax.ppermute(block, ("far", "chip", "core"), route)


plane = ("x", "z")


def update_kernel(scale, copied, here_ref, there_ref, state_ref, wide_out, state_out, sems):
    size = here_ref.shape[0]
    grad = (here_ref[...] + there_ref[...]) / scale
    vecs, sums = adagrad(state_ref[:size, :], state_ref[size:2 * size, :], grad)
    state_out[:size, :] = vecs
    state_out[size:2 * size, :] = sums
    state_out[2 * size:, :] = state_ref[2 * size:, :]
    copies = [
        pltpu.make_async_copy(state_out.at[pl.ds(0, copied * size)], wide_out.at[n], sems.at[n])
        for n in range(wide_out.shape[0])
    ]
    for copy in copies:
        copy.start()
    for copy in copies:
        copy.wait()


def updated(scale, copies, copied, here, there, state):
    size, cols = here.shape
    near = pl.BlockSpec(memory_space=pltpu.VMEM)
    return pl.pallas_call(
        functools.partial(update_kernel, scale, copied),
        in_specs=[near] * 3,
        out_specs=[pl.BlockSpec(memory_space=pltpu.HBM), near],
        out_shape=[
            jax.ShapeDtypeStruct((copies, copied * size, cols), f32),
            jax.ShapeDtypeStruct(state.shape, f32),
        ],
        scratch_shapes=[pltpu.SemaphoreType.DMA((copies,))],
        compiler_params=pltpu.CompilerParams(vmem_limit_bytes=vmem_small),
        name="update",
    )(here, there, state)


def row_update_kernel(scale, core_ref, mine_ref, other_ref, vecs_ref, sums_ref, vecs_out, sums_out):
    half = mine_ref.shape[0]
    for ref, n in ((mine_ref, core_ref[0]), (other_ref, 1 - core_ref[0])):
        span = pl.ds(pl.multiple_of(n * half, half), half)
        vecs, sums = adagrad(vecs_ref[span, :], sums_ref[span, :], ref[...] / scale)
        vecs_out[span, :] = vecs
        sums_out[span, :] = sums


def row_updated(scale, core, mine, other, vecs, sums):
    near = pl.BlockSpec(memory_space=pltpu.VMEM)
    return pl.pallas_call(
        functools.partial(row_update_kernel, scale),
        in_specs=[pl.BlockSpec(memory_space=pltpu.SMEM)] + [near] * 4,
        out_specs=[near] * 2,
        out_shape=[jax.ShapeDtypeStruct(vecs.shape, f32)] * 2,
        compiler_params=pltpu.CompilerParams(vmem_limit_bytes=2 * vmem_small),
        cost_estimate=pl.CostEstimate(flops=0, bytes_accessed=0, transcendentals=0),
        name="row_update",
    )(jnp.full((1,), core, jnp.int32), mine, other, vecs, sums)


def upright_kernel(spread_ref, vecs_ref, sums_ref):
    n, both, cols = spread_ref.shape
    size = both // 2
    vecs_ref[...] = spread_ref[:, :size].reshape(n * size, cols).T
    sums_ref[...] = spread_ref[:, size:].reshape(n * size, cols).T


def upright(spread):
    n, both, cols = spread.shape
    k = n * both // 2
    wide = pl.BlockSpec((tile, k), lambda c: (c, 0))
    like = jax.ShapeDtypeStruct((cols, k), f32)
    return pl.pallas_call(
        upright_kernel,
        grid=(cols // tile,),
        in_specs=[pl.BlockSpec((n, both, tile), lambda c: (0, 0, c))],
        out_specs=[wide, wide],
        out_shape=[like, like],
        compiler_params=pltpu.CompilerParams(vmem_limit_bytes=vmem_limit),
        name="upright",
    )(spread)


def shards(counts, row_embed, row_accum, col_embed, col_accum, row_log, col_log):
    row_vecs, row_sums = (row_embed, row_accum)
    col_vecs = col_embed
    row_bias = row_log.reshape(-1, 128)
    n_plane = lax.axis_size("x") * lax.axis_size("z")
    n_row = n_plane * lax.axis_size("far")
    n_col = lax.axis_size("chip") * lax.axis_size("core")
    row_scale = math.sqrt(n_col * col_embed.shape[0])
    col_scale = math.sqrt(n_row * row_embed.shape[0])
    cols, k = col_embed.shape
    size = k // n_plane
    me = lax.axis_index("x") * lax.axis_size("z") + lax.axis_index("z")
    core = lax.axis_index("core")
    state = jnp.concatenate(
        [lax.dynamic_slice_in_dim(v, me * size, size, 1).T for v in (col_embed, col_accum)]
        + [jnp.broadcast_to(col_log[None], (8, cols))],
        axis=0,
    )
    turns = counts.shape[0]
    for turn in range(turns):
        first, last = turn == 0, turn == turns - 1
        product, residual = residual_and_product(first, turn, counts, row_vecs, col_vecs, row_bias, state)
        terms = lax.all_to_all(product.reshape(n_plane, size, cols), plane, 0, 0)
        other = swap(row_part_of(first, 1 - core, residual, col_vecs), "core")
        mine = row_part_of(first, core, residual, col_vecs) + other
        if not last:
            state = to_next_place(state)
        terms, mine, state = lax.optimization_barrier((terms, mine, state))
        total = jnp.sum(terms, axis=0)
        if not last:
            here, there = to_next_place(total), to_next_place_and_far(total)
        else:
            here, there = total, swap(total, "far")
        here, there, mine = lax.optimization_barrier((here, there, mine))
        wide, state = updated(col_scale, n_plane, 2 if last else 1, here, there, state)
        spread = lax.all_to_all(wide, plane, 0, 0)
        mine = mine + swap(mine, "chip")
        if last:
            col_vecs, col_sums = upright(spread)
        else:
            col_vecs = spread.reshape(k, cols)
        row_vecs, row_sums = row_updated(row_scale, core, mine, swap(mine, "core"), row_vecs, row_sums)
    return (row_vecs, row_sums, col_vecs, col_sums)


def solution(mesh):
    fine = Mesh(mesh.devices.reshape(4, 4, 2, 2, 2), ("x", "z", "far", "chip", "core"))
    row = ("x", "z", "far")
    col = ("chip", "core")
    return jax.shard_map(
        shards,
        mesh=fine,
        in_specs=(
            P(None, row, col),
            P(row, None),
            P(row, None),
            P(col, None),
            P(col, None),
            P(row),
            P(col),
        ),
        out_specs=(P(row, None), P(row, None), P(col, None), P(col, None)),
        check_vma=False,
    )
```

time: 1290 us -> 198 us (0.15)
  waiting for transfers between devices: 1170 us -> 85.9 us
  matrix products: 73.8 us -> 0 us
  Pallas kernels: 0 us -> 53.1 us
  starting transfers between devices: 2.44 us -> 39.2 us
  between operations: 14.4 us -> 1.04 us
    psum x6 -> x0, waiting for transfers between devices: 1140 us -> none  [the longest x3 1040 us: shards(): col_total = lax.psum(product, 'row')]
    dot_general x9 -> x0, matrix products: 73.8 us -> none  [the longest x3 28.7 us: swivel_residual(): jnp.dot(row_vecs, col_vecs.T, precision=highest, preferred_element_type=j...]
    pallas_call x0 -> x16, Pallas kernels: none -> 53.1 us  [the longest x3 24.1 us: residual_and_product(): pl.pallas_call(functools.partial(residual_kernel, first, turn), in_specs=...]
    all_to_all x0 -> x6, waiting for transfers between devices: none -> 44.1 us  [the longest x3 25.8 us: shards(): terms = lax.all_to_all(product.reshape(n_plane, size, cols), plane, 0, 0)]
    all_to_all x0 -> x6, starting transfers between devices: none -> 27 us  [the longest x3 16 us: shards(): terms = lax.all_to_all(product.reshape(n_plane, size, cols), plane, 0, 0)]
    ppermute x6 -> x16, waiting for transfers between devices: 30.4 us -> 41.8 us  [the longest x10 32 us: swap(): return lax.ppermute(block, axis, [(i, i ^ 1) for i in range(n)])]
  transfers between devices with their start and end apart: 12 -> 22, of which waited for: 8 -> 19; matrix products, arithmetic and copies ran while one was open for 3% -> 1% of each run, Pallas kernels for 0% -> 12%
where the time goes in v2:
time: 198 us; the launch traced here: 195 us
  waiting for transfers between devices  85.9 us (43%)
  Pallas kernels  53.1 us (27%)
  starting transfers between devices  39.2 us (20%)
  local copies, waits for them, and re-layouts  10.4 us (5%)
  other arithmetic  4.89 us (2%)
    ppermute x10, waiting for transfers between devices, swap(): return lax.ppermute(block, axis, [(i, i ^ 1) for i in range(n)])  32 us
    all_to_all x3, waiting for transfers between devices, shards(): terms = lax.all_to_all(product.reshape(n_plane, size, cols), plane, 0, 0)  25.8 us
    pallas_call x3, Pallas kernels, residual_and_product(): pl.pallas_call(functools.partial(residual_kernel, first, turn), in_specs=...  24.1 us
    all_to_all x3, waiting for transfers between devices, shards(): spread = lax.all_to_all(wide, plane, 0, 0)  18.3 us
    pallas_call x6, Pallas kernels, row_part_of(): pl.pallas_call(functools.partial(row_part_kernel, first), grid_spec=pltpu...  18 us
    all_to_all x3, starting transfers between devices, shards(): terms = lax.all_to_all(product.reshape(n_plane, size, cols), plane, 0, 0)  16 us
    all_to_all x3, starting transfers between devices, shards(): spread = lax.all_to_all(wide, plane, 0, 0)  11.1 us
    ppermute x10, starting transfers between devices, swap(): return lax.ppermute(block, axis, [(i, i ^ 1) for i in range(n)])  9.33 us
  transfers between devices with their start and end apart: 22, of which 19 were waited for; matrix products, arithmetic and copies ran while one was open for 1% of the time, Pallas kernels for 12%

profile of v2, /device:TPU:8, one launch (start us, length us, event | category | flops | bytes accessed | tf_op | source)
XLA Modules:
  0.0 194.5 jit_solution(17660282728662978726)
XLA Ops:
  4.1 8.1 %residual.3 = (f32[256,1024]{1,0:T(8,128)}, f32[1024,1024]{1,0:T(8,128)}) custom-call(s32[3,1024,1024]{2,1,0:T(8,128)} %counts_ref.5, f32[1024,256]{1,0:T(8,128)S(1)} %copy-done.1, f32[1024,256]{1,0:T(8,128)S(1)} %copy-done, f32[8,128]{1,0:T(8,128)S(1)} %bitcast.16, f32[40,1024]{1,0:T(8,128)S(1)} %pad_maximum_fusion.state_in), custom_call_target="tpu_custom_call" | custom-call | tf_op jit(solution)/shard_map/residual/pallas_call | solution.py:117
  12.2 7.9 %all-to-all-start = ((f32[16,16,1024]{2,1,0:T(8,128)}), f32[16,16,1024]{2,1,0:T(8,128)}, u32[]{:S(2)}, u32[]{:S(2)}) async-start(f32[16,16,1024]{2,1,0:T(8,128)} %bitcast.4), calls=%async_computation | async-start | bytes 2097152 | tf_op jit(solution)/shard_map/all_to_all | solution.py:313
  28.0 9.9 %all-to-all-done = f32[16,16,1024]{2,1,0:T(8,128)} async-done(((f32[16,16,1024]{2,1,0:T(8,128)}), f32[16,16,1024]{2,1,0:T(8,128)}, u32[]{:S(2)}, u32[]{:S(2)}) %all-to-all-start) | async-done | bytes 1048608 | tf_op jit(solution)/shard_map/all_to_all | solution.py:313
  46.4 3.7 %all-to-all-start.1 = ((f32[16,16,1024]{2,1,0:T(8,128)}), f32[16,16,1024]{2,1,0:T(8,128)S(1)}, u32[]{:S(2)}, u32[]{:S(2)}) async-start(f32[16,16,1024]{2,1,0:T(8,128)} %get-tuple-element.50), calls=%async_computation.1 | async-start | bytes 2097152 | tf_op jit(solution)/shard_map/all_to_all | solution.py:326
  50.1 7.8 %collective-permute-done.4 = f32[512,256]{1,0:T(8,128)S(1)} collective-permute-done((f32[512,256]{1,0:T(8,128)S(1)}, f32[512,256]{1,0:T(8,128)S(1)}, u32[]{:S(2)}, u32[]{:S(2)}) %collective-permute-start.4) | collective-permute-done | bytes 524320 | tf_op jit(solution)/shard_map/ppermute | solution.py:193
  62.9 4.8 %all-to-all-done.1 = f32[16,16,1024]{2,1,0:T(8,128)S(1)} async-done(((f32[16,16,1024]{2,1,0:T(8,128)}), f32[16,16,1024]{2,1,0:T(8,128)S(1)}, u32[]{:S(2)}, u32[]{:S(2)}) %all-to-all-start.1) | async-done | bytes 1048608 | tf_op jit(solution)/shard_map/all_to_all | solution.py:326
  67.6 8.0 %residual.4 = (f32[256,1024]{1,0:T(8,128)}, f32[1024,1024]{1,0:T(8,128)}) custom-call(s32[3,1024,1024]{2,1,0:T(8,128)} %counts_ref.5, f32[1024,256]{1,0:T(8,128)S(1)} %get-tuple-element.46.row_in.vecs_ref, f32[256,1024]{1,0:T(8,128)S(1)} %bitcast.10, f32[8,128]{1,0:T(8,128)S(1)} %bitcast.17, f32[40,1024]{1,0:T(8,128)S(1)} %get-tuple-element.51.state_in), custom_call_target="tpu_custom_call" | custom-call | tf_op jit(solution)/shard_map/residual/pallas_call | solution.py:117
  75.7 4.4 %all-to-all-start.2 = ((f32[16,16,1024]{2,1,0:T(8,128)}), f32[16,16,1024]{2,1,0:T(8,128)}, u32[]{:S(2)}, u32[]{:S(2)}) async-start(f32[16,16,1024]{2,1,0:T(8,128)} %bitcast.7), calls=%async_computation.2 | async-start | bytes 2097152 | tf_op jit(solution)/shard_map/all_to_all | solution.py:313
  80.1 3.0 %row_part.9 = f32[512,256]{1,0:T(8,128)S(1)} custom-call(s32[1]{0:T(128)} %bitcast.5.half_ref, f32[1024,1024]{1,0:T(8,128)} %get-tuple-element.53.residual_ref, f32[256,1024]{1,0:T(8,128)S(1)} %bitcast.11), custom_call_target="tpu_custom_call" | custom-call | tf_op jit(solution)/shard_map/row_part/pallas_call | solution.py:167
  88.0 7.2 %all-to-all-done.2 = f32[16,16,1024]{2,1,0:T(8,128)} async-done(((f32[16,16,1024]{2,1,0:T(8,128)}), f32[16,16,1024]{2,1,0:T(8,128)}, u32[]{:S(2)}, u32[]{:S(2)}) %all-to-all-start.2) | async-done | bytes 1048608 | tf_op jit(solution)/shard_map/all_to_all | solution.py:313
  96.6 3.6 %collective-permute-done.9.there_ref = f32[16,1024]{1,0:T(8,128)S(1)} collective-permute-done((f32[16,1024]{1,0:T(8,128)S(1)}, f32[16,1024]{1,0:T(8,128)S(1)}, u32[]{:S(2)}, u32[]{:S(2)}) %collective-permute-start.9) | collective-permute-done | bytes 65568 | tf_op jit(solution)/shard_map/ppermute | solution.py:206
  103.6 3.7 %all-to-all-start.3 = ((f32[16,16,1024]{2,1,0:T(8,128)}), f32[16,16,1024]{2,1,0:T(8,128)S(1)}, u32[]{:S(2)}, u32[]{:S(2)}) async-start(f32[16,16,1024]{2,1,0:T(8,128)} %get-tuple-element.62), calls=%async_computation.3 | async-start | bytes 2097152 | tf_op jit(solution)/shard_map/all_to_all | solution.py:326
  107.2 5.7 %collective-permute-done.10 = f32[512,256]{1,0:T(8,128)S(1)} collective-permute-done((f32[512,256]{1,0:T(8,128)S(1)}, f32[512,256]{1,0:T(8,128)S(1)}, u32[]{:S(2)}, u32[]{:S(2)}) %collective-permute-start.10) | collective-permute-done | bytes 524320 | tf_op jit(solution)/shard_map/ppermute | solution.py:193
  118.0 4.6 %all-to-all-done.3 = f32[16,16,1024]{2,1,0:T(8,128)S(1)} async-done(((f32[16,16,1024]{2,1,0:T(8,128)}), f32[16,16,1024]{2,1,0:T(8,128)S(1)}, u32[]{:S(2)}, u32[]{:S(2)}) %all-to-all-start.3) | async-done | bytes 1048608 | tf_op jit(solution)/shard_map/all_to_all | solution.py:326
  122.6 8.0 %residual.5 = (f32[256,1024]{1,0:T(8,128)}, f32[1024,1024]{1,0:T(8,128)}) custom-call(s32[3,1024,1024]{2,1,0:T(8,128)} %counts_ref.5, f32[1024,256]{1,0:T(8,128)S(1)} %get-tuple-element.58.row_in.vecs_ref, f32[256,1024]{1,0:T(8,128)S(1)} %bitcast.13, f32[8,128]{1,0:T(8,128)S(1)} %bitcast.18, f32[40,1024]{1,0:T(8,128)S(1)} %get-tuple-element.74.state_in.state_ref), custom_call_target="tpu_custom_call" | custom-call | tf_op jit(solution)/shard_map/residual/pallas_call | solution.py:117
  130.6 3.7 %all-to-all-start.4 = ((f32[16,16,1024]{2,1,0:T(8,128)}), f32[16,16,1024]{2,1,0:T(8,128)S(1)}, u32[]{:S(2)}, u32[]{:S(2)}) async-start(f32[16,16,1024]{2,1,0:T(8,128)} %bitcast.9), calls=%async_computation.4 | async-start | bytes 2097152 | tf_op jit(solution)/shard_map/all_to_all | solution.py:313
  137.4 3.0 %row_part.10 = f32[512,256]{1,0:T(8,128)S(1)} custom-call(s32[1]{0:T(128)} %bitcast.half_ref.core_ref, f32[1024,1024]{1,0:T(8,128)} %get-tuple-element.65.residual_ref, f32[256,1024]{1,0:T(8,128)S(1)} %bitcast.15), custom_call_target="tpu_custom_call" | custom-call | tf_op jit(solution)/shard_map/row_part/pallas_call | solution.py:167
  141.4 8.8 %all-to-all-done.4 = f32[16,16,1024]{2,1,0:T(8,128)S(1)} async-done(((f32[16,16,1024]{2,1,0:T(8,128)}), f32[16,16,1024]{2,1,0:T(8,128)S(1)}, u32[]{:S(2)}, u32[]{:S(2)}) %all-to-all-start.4) | async-done | bytes 1048608 | tf_op jit(solution)/shard_map/all_to_all | solution.py:313
  152.2 3.8 %collective-permute-done.13.there_ref = f32[16,1024]{1,0:T(8,128)S(1)} collective-permute-done((f32[16,1024]{1,0:T(8,128)S(1)}, f32[16,1024]{1,0:T(8,128)S(1)}, u32[]{:S(2)}, u32[]{:S(2)}) %collective-permute-start.13) | collective-permute-done | bytes 65568 | tf_op jit(solution)/shard_map/ppermute | solution.py:193
  156.0 3.6 %update.5 = (f32[16,32,1024]{2,1,0:T(8,128)S(1)}, f32[40,1024]{1,0:T(8,128)}) custom-call(f32[16,1024]{1,0:T(8,128)S(1)} %reduce_sum.29.here_ref, f32[16,1024]{1,0:T(8,128)S(1)} %collective-permute-done.13.there_ref, f32[40,1024]{1,0:T(8,128)S(1)} %get-tuple-element.74.state_in.state_ref), custom_call_target="tpu_custom_call" | custom-call | tf_op jit(solution)/shard_map/update/pallas_call | solution.py:232
  161.0 3.7 %all-to-all-start.5 = ((f32[16,32,1024]{2,1,0:T(8,128)}), f32[16,32,1024]{2,1,0:T(8,128)S(1)}, u32[]{:S(2)}, u32[]{:S(2)}) async-start(f32[16,32,1024]{2,1,0:T(8,128)} %copy-done.4), calls=%async_computation.5 | async-start | bytes 4194304 | tf_op jit(solution)/shard_map/all_to_all | solution.py:326
  164.7 3.5 %collective-permute-start.14 = (f32[512,256]{1,0:T(8,128)}, f32[512,256]{1,0:T(8,128)S(1)}, u32[]{:S(2)}, u32[]{:S(2)}) collective-permute-start(f32[512,256]{1,0:T(8,128)} %add.31), channel_id=1, source_target_pairs={{0,2},{2,0},{1,3},{3,1},{4,6},{6,4},{5,7},{7,5},{8,10},{10,8},{9,1... | collective-permute-start | bytes 1572872 | tf_op jit(solution)/shard_map/ppermute | solution.py:193
  168.2 9.0 %collective-permute-done.14 = f32[512,256]{1,0:T(8,128)S(1)} collective-permute-done((f32[512,256]{1,0:T(8,128)}, f32[512,256]{1,0:T(8,128)S(1)}, u32[]{:S(2)}, u32[]{:S(2)}) %collective-permute-start.14) | collective-permute-done | bytes 524320 | tf_op jit(solution)/shard_map/ppermute | solution.py:193
  183.4 8.9 %all-to-all-done.5.spread_ref = f32[16,32,1024]{2,1,0:T(8,128)S(1)} async-done(((f32[16,32,1024]{2,1,0:T(8,128)}), f32[16,32,1024]{2,1,0:T(8,128)S(1)}, u32[]{:S(2)}, u32[]{:S(2)}) %all-to-all-start.5) | async-done | bytes 2097184 | tf_op jit(solution)/shard_map/all_to_all | solution.py:326
  (74 shorter events, 55.2 us)
Async XLA Ops:
  12.2 25.7 %all-to-all-start = ((f32[16,16,1024]{2,1,0:T(8,128)}), f32[16,16,1024]{2,1,0:T(8,128)}, u32[]{:S(2)}, u32[]{:S(2)}) async-start(f32[16,16,1024]{2,1,0:T(8,128)} %bitcast.4), calls=%async_computation | async-start | bytes 2097152 | tf_op jit(solution)/shard_map/all_to_all | solution.py:313
  23.1 3.5 %collective-permute-start = (f32[512,256]{1,0:T(8,128)S(1)}, f32[512,256]{1,0:T(8,128)S(1)}, u32[]{:S(2)}, u32[]{:S(2)}) collective-permute-start(f32[512,256]{1,0:T(8,128)S(1)} %row_part.7), channel_id=1, source_target_pairs={{0,1},{1,0},{2,3},{3,2},{4,5},{5,4},{6,7},{7,6},{8,9},{9,8},{10,11... | collective-permute-start | bytes 1572872 | tf_op jit(solution)/shard_map/ppermute | solution.py:193
  23.2 4.8 %collective-permute-start.1 = (f32[40,1024]{1,0:T(8,128)S(1)}, f32[40,1024]{1,0:T(8,128)S(1)}, u32[]{:S(2)}, u32[]{:S(2)}) collective-permute-start(f32[40,1024]{1,0:T(8,128)S(1)} %pad_maximum_fusion.state_in), channel_id=1, source_target_pairs={{0,1},{1,2},{2,3},{3,0},{4,5},{5,6},{6,7},{7,4},{8,9},{9,10},{10,1... | collective-permute-start | bytes 491528 | tf_op jit(solution)/shard_map/ppermute | solution.py:199
  26.7 40.9 %copy-start.11 = (f32[1024]{0:T(1024)S(1)}, f32[1024]{0:T(1024)}, u32[]{:S(2)}) copy-start(f32[1024]{0:T(1024)} %param.12) | copy-start | bytes 12292
  39.2 3.8 %collective-permute-start.3 = (f32[16,1024]{1,0:T(8,128)S(1)}, f32[16,1024]{1,0:T(8,128)S(1)}, u32[]{:S(2)}, u32[]{:S(2)}) collective-permute-start(f32[16,1024]{1,0:T(8,128)S(1)} %reduce_sum.27), channel_id=1, source_target_pairs={{0,5},{1,6},{2,7},{3,4},{4,1},{5,2},{6,3},{7,0},{8,13},{9,14},{10,... | collective-permute-start | bytes 196616 | tf_op jit(solution)/shard_map/ppermute | solution.py:206
  39.3 5.1 %collective-permute-start.2 = (f32[16,1024]{1,0:T(8,128)S(1)}, f32[16,1024]{1,0:T(8,128)S(1)}, u32[]{:S(2)}, u32[]{:S(2)}) collective-permute-start(f32[16,1024]{1,0:T(8,128)S(1)} %reduce_sum.27), channel_id=1, source_target_pairs={{0,1},{1,2},{2,3},{3,0},{4,5},{5,6},{6,7},{7,4},{8,9},{9,10},{10,1... | collective-permute-start | bytes 196616 | tf_op jit(solution)/shard_map/ppermute | solution.py:199
  44.4 13.5 %collective-permute-start.4 = (f32[512,256]{1,0:T(8,128)S(1)}, f32[512,256]{1,0:T(8,128)S(1)}, u32[]{:S(2)}, u32[]{:S(2)}) collective-permute-start(f32[512,256]{1,0:T(8,128)S(1)} %add.27), channel_id=1, source_target_pairs={{0,2},{2,0},{1,3},{3,1},{4,6},{6,4},{5,7},{7,5},{8,10},{10,8},{9,1... | collective-permute-start | bytes 1572872 | tf_op jit(solution)/shard_map/ppermute | solution.py:193
  46.4 21.2 %all-to-all-start.1 = ((f32[16,16,1024]{2,1,0:T(8,128)}), f32[16,16,1024]{2,1,0:T(8,128)S(1)}, u32[]{:S(2)}, u32[]{:S(2)}) async-start(f32[16,16,1024]{2,1,0:T(8,128)} %get-tuple-element.50), calls=%async_computation.1 | async-start | bytes 2097152 | tf_op jit(solution)/shard_map/all_to_all | solution.py:326
  58.0 2.2 %collective-permute-start.5 = (f32[512,256]{1,0:T(8,128)S(1)}, f32[512,256]{1,0:T(8,128)S(1)}, u32[]{:S(2)}, u32[]{:S(2)}) collective-permute-start(f32[512,256]{1,0:T(8,128)S(1)} %add.28.mine_ref), channel_id=1, source_target_pairs={{0,1},{1,0},{2,3},{3,2},{4,5},{5,4},{6,7},{7,6},{8,9},{9,8},{10,11... | collective-permute-start | bytes 1572872 | tf_op jit(solution)/shard_map/ppermute | solution.py:193
  75.7 19.5 %all-to-all-start.2 = ((f32[16,16,1024]{2,1,0:T(8,128)}), f32[16,16,1024]{2,1,0:T(8,128)}, u32[]{:S(2)}, u32[]{:S(2)}) async-start(f32[16,16,1024]{2,1,0:T(8,128)} %bitcast.7), calls=%async_computation.2 | async-start | bytes 2097152 | tf_op jit(solution)/shard_map/all_to_all | solution.py:313
  83.1 3.6 %collective-permute-start.6 = (f32[512,256]{1,0:T(8,128)S(1)}, f32[512,256]{1,0:T(8,128)S(1)}, u32[]{:S(2)}, u32[]{:S(2)}) collective-permute-start(f32[512,256]{1,0:T(8,128)S(1)} %row_part.9), channel_id=1, source_target_pairs={{0,1},{1,0},{2,3},{3,2},{4,5},{5,4},{6,7},{7,6},{8,9},{9,8},{10,11... | collective-permute-start | bytes 1572872 | tf_op jit(solution)/shard_map/ppermute | solution.py:193
  83.2 4.8 %collective-permute-start.7 = (f32[40,1024]{1,0:T(8,128)S(1)}, f32[40,1024]{1,0:T(8,128)S(1)}, u32[]{:S(2)}, u32[]{:S(2)}) collective-permute-start(f32[40,1024]{1,0:T(8,128)S(1)} %get-tuple-element.51.state_in), channel_id=1, source_target_pairs={{0,1},{1,2},{2,3},{3,0},{4,5},{5,6},{6,7},{7,4},{8,9},{9,10},{10,1... | collective-permute-start | bytes 491528 | tf_op jit(solution)/shard_map/ppermute | solution.py:199
  96.5 3.8 %collective-permute-start.9 = (f32[16,1024]{1,0:T(8,128)S(1)}, f32[16,1024]{1,0:T(8,128)S(1)}, u32[]{:S(2)}, u32[]{:S(2)}) collective-permute-start(f32[16,1024]{1,0:T(8,128)S(1)} %reduce_sum.28), channel_id=1, source_target_pairs={{0,5},{1,6},{2,7},{3,4},{4,1},{5,2},{6,3},{7,0},{8,13},{9,14},{10,... | collective-permute-start | bytes 196616 | tf_op jit(solution)/shard_map/ppermute | solution.py:206
  96.5 3.9 %collective-permute-start.8 = (f32[16,1024]{1,0:T(8,128)S(1)}, f32[16,1024]{1,0:T(8,128)S(1)}, u32[]{:S(2)}, u32[]{:S(2)}) collective-permute-start(f32[16,1024]{1,0:T(8,128)S(1)} %reduce_sum.28), channel_id=1, source_target_pairs={{0,1},{1,2},{2,3},{3,0},{4,5},{5,6},{6,7},{7,4},{8,9},{9,10},{10,1... | collective-permute-start | bytes 196616 | tf_op jit(solution)/shard_map/ppermute | solution.py:199
  100.5 12.5 %collective-permute-start.10 = (f32[512,256]{1,0:T(8,128)S(1)}, f32[512,256]{1,0:T(8,128)S(1)}, u32[]{:S(2)}, u32[]{:S(2)}) collective-permute-start(f32[512,256]{1,0:T(8,128)S(1)} %add.29), channel_id=1, source_target_pairs={{0,2},{2,0},{1,3},{3,1},{4,6},{6,4},{5,7},{7,5},{8,10},{10,8},{9,1... | collective-permute-start | bytes 1572872 | tf_op jit(solution)/shard_map/ppermute | solution.py:193
  103.6 19.0 %all-to-all-start.3 = ((f32[16,16,1024]{2,1,0:T(8,128)}), f32[16,16,1024]{2,1,0:T(8,128)S(1)}, u32[]{:S(2)}, u32[]{:S(2)}) async-start(f32[16,16,1024]{2,1,0:T(8,128)} %get-tuple-element.62), calls=%async_computation.3 | async-start | bytes 2097152 | tf_op jit(solution)/shard_map/all_to_all | solution.py:326
  113.0 2.2 %collective-permute-start.11 = (f32[512,256]{1,0:T(8,128)S(1)}, f32[512,256]{1,0:T(8,128)S(1)}, u32[]{:S(2)}, u32[]{:S(2)}) collective-permute-start(f32[512,256]{1,0:T(8,128)S(1)} %add.30.mine_ref), channel_id=1, source_target_pairs={{0,1},{1,0},{2,3},{3,2},{4,5},{5,4},{6,7},{7,6},{8,9},{9,8},{10,11... | collective-permute-start | bytes 1572872 | tf_op jit(solution)/shard_map/ppermute | solution.py:193
  130.6 19.5 %all-to-all-start.4 = ((f32[16,16,1024]{2,1,0:T(8,128)}), f32[16,16,1024]{2,1,0:T(8,128)S(1)}, u32[]{:S(2)}, u32[]{:S(2)}) async-start(f32[16,16,1024]{2,1,0:T(8,128)} %bitcast.9), calls=%async_computation.4 | async-start | bytes 2097152 | tf_op jit(solution)/shard_map/all_to_all | solution.py:313
  137.3 3.1 %collective-permute-start.12 = (f32[512,256]{1,0:T(8,128)S(1)}, f32[512,256]{1,0:T(8,128)S(1)}, u32[]{:S(2)}, u32[]{:S(2)}) collective-permute-start(f32[512,256]{1,0:T(8,128)S(1)} %row_part.11), channel_id=1, source_target_pairs={{0,1},{1,0},{2,3},{3,2},{4,5},{5,4},{6,7},{7,6},{8,9},{9,8},{10,11... | collective-permute-start | bytes 1572872 | tf_op jit(solution)/shard_map/ppermute | solution.py:193
  140.5 39.8 %copy-start.3 = (f32[1024,256]{1,0:T(8,128)S(1)}, f32[1024,256]{1,0:T(8,128)}, u32[]{:S(2)}) copy-start(f32[1024,256]{1,0:T(8,128)} %copy-done.2) | copy-start | bytes 3145732
  150.2 5.8 %collective-permute-start.13 = (f32[16,1024]{1,0:T(8,128)S(1)}, f32[16,1024]{1,0:T(8,128)S(1)}, u32[]{:S(2)}, u32[]{:S(2)}) collective-permute-start(f32[16,1024]{1,0:T(8,128)S(1)} %reduce_sum.29.here_ref), channel_id=1, source_target_pairs={{0,4},{4,0},{1,5},{5,1},{2,6},{6,2},{3,7},{7,3},{8,12},{12,8},{9,1... | collective-permute-start | bytes 196616 | tf_op jit(solution)/shard_map/ppermute | solution.py:193
  161.0 31.4 %all-to-all-start.5 = ((f32[16,32,1024]{2,1,0:T(8,128)}), f32[16,32,1024]{2,1,0:T(8,128)S(1)}, u32[]{:S(2)}, u32[]{:S(2)}) async-start(f32[16,32,1024]{2,1,0:T(8,128)} %copy-done.4), calls=%async_computation.5 | async-start | bytes 4194304 | tf_op jit(solution)/shard_map/all_to_all | solution.py:326
  164.7 12.5 %collective-permute-start.14 = (f32[512,256]{1,0:T(8,128)}, f32[512,256]{1,0:T(8,128)S(1)}, u32[]{:S(2)}, u32[]{:S(2)}) collective-permute-start(f32[512,256]{1,0:T(8,128)} %add.31), channel_id=1, source_target_pairs={{0,2},{2,0},{1,3},{3,1},{4,6},{6,4},{5,7},{7,5},{8,10},{10,8},{9,1... | collective-permute-start | bytes 1572872 | tf_op jit(solution)/shard_map/ppermute | solution.py:193
  178.3 2.0 %collective-permute-start.15 = (f32[512,256]{1,0:T(8,128)S(1)}, f32[512,256]{1,0:T(8,128)S(1)}, u32[]{:S(2)}, u32[]{:S(2)}) collective-permute-start(f32[512,256]{1,0:T(8,128)S(1)} %add.32.mine_ref), channel_id=1, source_target_pairs={{0,1},{1,0},{2,3},{3,2},{4,5},{5,4},{6,7},{7,6},{8,9},{9,8},{10,11... | collective-permute-start | bytes 1572872 | tf_op jit(solution)/shard_map/ppermute | solution.py:193
  (10 other events, 25.9 us)

commit v3 on v2

--- a/solution.py
+++ b/solution.py
@@ -12,6 +12,7 @@
 f32 = jnp.float32
 bf16 = jnp.bfloat16
 tile = 256
+chunk = 512
 vmem_limit = 50 * 2**20
 vmem_most = 50 * 2**20
 vmem_small = 8 * 2**20
@@ -58,7 +59,7 @@
     ]
     for load in loads:
         load.start()
-    spans = [pl.ds(t * tile, tile) for t in range(rows // tile)]
+    spans = [pl.ds(t * chunk, chunk) for t in range(rows // chunk)]
     fetches = [
         pltpu.make_async_copy(counts_ref.at[turn, span, :], block_ref.at[span, :], block_sems.at[t])
         for t, span in enumerate(spans)
@@ -73,7 +74,7 @@
     for t, span in enumerate(spans):
         for n, v in enumerate(parts(row_ref[span, :], 3)):
             if n < 2:
-                row_parts[pl.ds(n * rows + t * tile, tile), :] = v
+                row_parts[pl.ds(n * rows + t * chunk, chunk), :] = v
             rowt_parts[pl.ds(n * k, k), span] = v.T
     loads[2].wait()
     for t in range(rows // 128):
@@ -112,7 +113,7 @@
 def residual_and_product(first, turn, counts, row_vecs, col_vecs, row_bias, state):
     _, rows, cols = counts.shape
     k = row_vecs.shape[1]
-    steps = rows // tile
+    steps = rows // chunk
     far = pl.BlockSpec(memory_space=pltpu.HBM)
     return pl.pallas_call(
         functools.partial(residual_kernel, first, turn),

time: 198 us -> 197 us (level)
  no operation moved by 1% of the time
where the time goes in v3:
time: 197 us; the launch traced here: 193 us
  waiting for transfers between devices  85.9 us (44%)
  Pallas kernels  51.9 us (26%)
  starting transfers between devices  39.2 us (20%)
  local copies, waits for them, and re-layouts  10.4 us (5%)
  other arithmetic  4.89 us (2%)
    ppermute x10, waiting for transfers between devices, swap(): return lax.ppermute(block, axis, [(i, i ^ 1) for i in range(n)])  31.9 us
    all_to_all x3, waiting for transfers between devices, shards(): terms = lax.all_to_all(product.reshape(n_plane, size, cols), plane, 0, 0)  25.8 us
    pallas_call x3, Pallas kernels, residual_and_product(): pl.pallas_call(functools.partial(residual_kernel, first, turn), in_specs=...  22.9 us
    all_to_all x3, waiting for transfers between devices, shards(): spread = lax.all_to_all(wide, plane, 0, 0)  18.5 us
    pallas_call x6, Pallas kernels, row_part_of(): pl.pallas_call(functools.partial(row_part_kernel, first), grid_spec=pltpu...  18 us
    all_to_all x3, starting transfers between devices, shards(): terms = lax.all_to_all(product.reshape(n_plane, size, cols), plane, 0, 0)  16 us
    all_to_all x3, starting transfers between devices, shards(): spread = lax.all_to_all(wide, plane, 0, 0)  11.1 us
    ppermute x10, starting transfers between devices, swap(): return lax.ppermute(block, axis, [(i, i ^ 1) for i in range(n)])  9.29 us
  transfers between devices with their start and end apart: 22, of which 19 were waited for; matrix products, arithmetic and copies ran while one was open for 1% of the time, Pallas kernels for 12%

profile of v3, /device:TPU:8, one launch (start us, length us, event | category | flops | bytes accessed | tf_op | source)
XLA Modules:
  0.0 193.3 jit_solution(7624233705044154903)
XLA Ops:
  4.1 7.7 %residual.3 = (f32[256,1024]{1,0:T(8,128)}, f32[1024,1024]{1,0:T(8,128)}) custom-call(s32[3,1024,1024]{2,1,0:T(8,128)} %counts_ref.5, f32[1024,256]{1,0:T(8,128)S(1)} %copy-done.1, f32[1024,256]{1,0:T(8,128)S(1)} %copy-done, f32[8,128]{1,0:T(8,128)S(1)} %bitcast.16, f32[40,1024]{1,0:T(8,128)S(1)} %pad_maximum_fusion.state_in), custom_call_target="tpu_custom_call" | custom-call | tf_op jit(solution)/shard_map/residual/pallas_call | solution.py:118
  11.8 7.9 %all-to-all-start = ((f32[16,16,1024]{2,1,0:T(8,128)}), f32[16,16,1024]{2,1,0:T(8,128)}, u32[]{:S(2)}, u32[]{:S(2)}) async-start(f32[16,16,1024]{2,1,0:T(8,128)} %bitcast.4), calls=%async_computation | async-start | bytes 2097152 | tf_op jit(solution)/shard_map/all_to_all | solution.py:314
  27.6 9.9 %all-to-all-done = f32[16,16,1024]{2,1,0:T(8,128)} async-done(((f32[16,16,1024]{2,1,0:T(8,128)}), f32[16,16,1024]{2,1,0:T(8,128)}, u32[]{:S(2)}, u32[]{:S(2)}) %all-to-all-start) | async-done | bytes 1048608 | tf_op jit(solution)/shard_map/all_to_all | solution.py:314
  46.1 3.7 %all-to-all-start.1 = ((f32[16,16,1024]{2,1,0:T(8,128)}), f32[16,16,1024]{2,1,0:T(8,128)S(1)}, u32[]{:S(2)}, u32[]{:S(2)}) async-start(f32[16,16,1024]{2,1,0:T(8,128)} %get-tuple-element.50), calls=%async_computation.1 | async-start | bytes 2097152 | tf_op jit(solution)/shard_map/all_to_all | solution.py:327
  49.7 7.7 %collective-permute-done.4 = f32[512,256]{1,0:T(8,128)S(1)} collective-permute-done((f32[512,256]{1,0:T(8,128)S(1)}, f32[512,256]{1,0:T(8,128)S(1)}, u32[]{:S(2)}, u32[]{:S(2)}) %collective-permute-start.4) | collective-permute-done | bytes 524320 | tf_op jit(solution)/shard_map/ppermute | solution.py:194
  62.4 4.7 %all-to-all-done.1 = f32[16,16,1024]{2,1,0:T(8,128)S(1)} async-done(((f32[16,16,1024]{2,1,0:T(8,128)}), f32[16,16,1024]{2,1,0:T(8,128)S(1)}, u32[]{:S(2)}, u32[]{:S(2)}) %all-to-all-start.1) | async-done | bytes 1048608 | tf_op jit(solution)/shard_map/all_to_all | solution.py:327
  67.2 7.6 %residual.4 = (f32[256,1024]{1,0:T(8,128)}, f32[1024,1024]{1,0:T(8,128)}) custom-call(s32[3,1024,1024]{2,1,0:T(8,128)} %counts_ref.5, f32[1024,256]{1,0:T(8,128)S(1)} %get-tuple-element.46.row_in.vecs_ref, f32[256,1024]{1,0:T(8,128)S(1)} %bitcast.10, f32[8,128]{1,0:T(8,128)S(1)} %bitcast.17, f32[40,1024]{1,0:T(8,128)S(1)} %get-tuple-element.51.state_in), custom_call_target="tpu_custom_call" | custom-call | tf_op jit(solution)/shard_map/residual/pallas_call | solution.py:118
  74.8 4.4 %all-to-all-start.2 = ((f32[16,16,1024]{2,1,0:T(8,128)}), f32[16,16,1024]{2,1,0:T(8,128)}, u32[]{:S(2)}, u32[]{:S(2)}) async-start(f32[16,16,1024]{2,1,0:T(8,128)} %bitcast.7), calls=%async_computation.2 | async-start | bytes 2097152 | tf_op jit(solution)/shard_map/all_to_all | solution.py:314
  87.1 7.2 %all-to-all-done.2 = f32[16,16,1024]{2,1,0:T(8,128)} async-done(((f32[16,16,1024]{2,1,0:T(8,128)}), f32[16,16,1024]{2,1,0:T(8,128)}, u32[]{:S(2)}, u32[]{:S(2)}) %all-to-all-start.2) | async-done | bytes 1048608 | tf_op jit(solution)/shard_map/all_to_all | solution.py:314
  95.8 3.6 %collective-permute-done.9.there_ref = f32[16,1024]{1,0:T(8,128)S(1)} collective-permute-done((f32[16,1024]{1,0:T(8,128)S(1)}, f32[16,1024]{1,0:T(8,128)S(1)}, u32[]{:S(2)}, u32[]{:S(2)}) %collective-permute-start.9) | collective-permute-done | bytes 65568 | tf_op jit(solution)/shard_map/ppermute | solution.py:207
  102.7 3.7 %all-to-all-start.3 = ((f32[16,16,1024]{2,1,0:T(8,128)}), f32[16,16,1024]{2,1,0:T(8,128)S(1)}, u32[]{:S(2)}, u32[]{:S(2)}) async-start(f32[16,16,1024]{2,1,0:T(8,128)} %get-tuple-element.62), calls=%async_computation.3 | async-start | bytes 2097152 | tf_op jit(solution)/shard_map/all_to_all | solution.py:327
  106.4 5.7 %collective-permute-done.10 = f32[512,256]{1,0:T(8,128)S(1)} collective-permute-done((f32[512,256]{1,0:T(8,128)S(1)}, f32[512,256]{1,0:T(8,128)S(1)}, u32[]{:S(2)}, u32[]{:S(2)}) %collective-permute-start.10) | collective-permute-done | bytes 524320 | tf_op jit(solution)/shard_map/ppermute | solution.py:194
  117.1 4.6 %all-to-all-done.3 = f32[16,16,1024]{2,1,0:T(8,128)S(1)} async-done(((f32[16,16,1024]{2,1,0:T(8,128)}), f32[16,16,1024]{2,1,0:T(8,128)S(1)}, u32[]{:S(2)}, u32[]{:S(2)}) %all-to-all-start.3) | async-done | bytes 1048608 | tf_op jit(solution)/shard_map/all_to_all | solution.py:327
  121.8 7.6 %residual.5 = (f32[256,1024]{1,0:T(8,128)}, f32[1024,1024]{1,0:T(8,128)}) custom-call(s32[3,1024,1024]{2,1,0:T(8,128)} %counts_ref.5, f32[1024,256]{1,0:T(8,128)S(1)} %get-tuple-element.58.row_in.vecs_ref, f32[256,1024]{1,0:T(8,128)S(1)} %bitcast.13, f32[8,128]{1,0:T(8,128)S(1)} %bitcast.18, f32[40,1024]{1,0:T(8,128)S(1)} %get-tuple-element.74.state_in.state_ref), custom_call_target="tpu_custom_call" | custom-call | tf_op jit(solution)/shard_map/residual/pallas_call | solution.py:118
  129.4 3.7 %all-to-all-start.4 = ((f32[16,16,1024]{2,1,0:T(8,128)}), f32[16,16,1024]{2,1,0:T(8,128)S(1)}, u32[]{:S(2)}, u32[]{:S(2)}) async-start(f32[16,16,1024]{2,1,0:T(8,128)} %bitcast.9), calls=%async_computation.4 | async-start | bytes 2097152 | tf_op jit(solution)/shard_map/all_to_all | solution.py:314
  133.1 3.0 %row_part.11 = f32[512,256]{1,0:T(8,128)S(1)} custom-call(s32[1]{0:T(128)} %bitcast.5.half_ref, f32[1024,1024]{1,0:T(8,128)} %get-tuple-element.65.residual_ref, f32[256,1024]{1,0:T(8,128)S(1)} %bitcast.14), custom_call_target="tpu_custom_call" | custom-call | tf_op jit(solution)/shard_map/row_part/pallas_call | solution.py:168
  136.2 3.0 %row_part.10 = f32[512,256]{1,0:T(8,128)S(1)} custom-call(s32[1]{0:T(128)} %bitcast.half_ref.core_ref, f32[1024,1024]{1,0:T(8,128)} %get-tuple-element.65.residual_ref, f32[256,1024]{1,0:T(8,128)S(1)} %bitcast.15), custom_call_target="tpu_custom_call" | custom-call | tf_op jit(solution)/shard_map/row_part/pallas_call | solution.py:168
  140.1 8.8 %all-to-all-done.4 = f32[16,16,1024]{2,1,0:T(8,128)S(1)} async-done(((f32[16,16,1024]{2,1,0:T(8,128)}), f32[16,16,1024]{2,1,0:T(8,128)S(1)}, u32[]{:S(2)}, u32[]{:S(2)}) %all-to-all-start.4) | async-done | bytes 1048608 | tf_op jit(solution)/shard_map/all_to_all | solution.py:314
  151.0 3.8 %collective-permute-done.13.there_ref = f32[16,1024]{1,0:T(8,128)S(1)} collective-permute-done((f32[16,1024]{1,0:T(8,128)S(1)}, f32[16,1024]{1,0:T(8,128)S(1)}, u32[]{:S(2)}, u32[]{:S(2)}) %collective-permute-start.13) | collective-permute-done | bytes 65568 | tf_op jit(solution)/shard_map/ppermute | solution.py:194
  154.8 3.6 %update.5 = (f32[16,32,1024]{2,1,0:T(8,128)S(1)}, f32[40,1024]{1,0:T(8,128)}) custom-call(f32[16,1024]{1,0:T(8,128)S(1)} %reduce_sum.29.here_ref, f32[16,1024]{1,0:T(8,128)S(1)} %collective-permute-done.13.there_ref, f32[40,1024]{1,0:T(8,128)S(1)} %get-tuple-element.74.state_in.state_ref), custom_call_target="tpu_custom_call" | custom-call | tf_op jit(solution)/shard_map/update/pallas_call | solution.py:233
  159.8 3.7 %all-to-all-start.5 = ((f32[16,32,1024]{2,1,0:T(8,128)}), f32[16,32,1024]{2,1,0:T(8,128)S(1)}, u32[]{:S(2)}, u32[]{:S(2)}) async-start(f32[16,32,1024]{2,1,0:T(8,128)} %copy-done.4), calls=%async_computation.5 | async-start | bytes 4194304 | tf_op jit(solution)/shard_map/all_to_all | solution.py:327
  163.5 3.4 %collective-permute-start.14 = (f32[512,256]{1,0:T(8,128)}, f32[512,256]{1,0:T(8,128)S(1)}, u32[]{:S(2)}, u32[]{:S(2)}) collective-permute-start(f32[512,256]{1,0:T(8,128)} %add.31), channel_id=1, source_target_pairs={{0,2},{2,0},{1,3},{3,1},{4,6},{6,4},{5,7},{7,5},{8,10},{10,8},{9,1... | collective-permute-start | bytes 1572872 | tf_op jit(solution)/shard_map/ppermute | solution.py:194
  166.9 8.9 %collective-permute-done.14 = f32[512,256]{1,0:T(8,128)S(1)} collective-permute-done((f32[512,256]{1,0:T(8,128)}, f32[512,256]{1,0:T(8,128)S(1)}, u32[]{:S(2)}, u32[]{:S(2)}) %collective-permute-start.14) | collective-permute-done | bytes 524320 | tf_op jit(solution)/shard_map/ppermute | solution.py:194
  182.0 9.1 %all-to-all-done.5.spread_ref = f32[16,32,1024]{2,1,0:T(8,128)S(1)} async-done(((f32[16,32,1024]{2,1,0:T(8,128)}), f32[16,32,1024]{2,1,0:T(8,128)S(1)}, u32[]{:S(2)}, u32[]{:S(2)}) %all-to-all-start.5) | async-done | bytes 2097184 | tf_op jit(solution)/shard_map/all_to_all | solution.py:327
  (74 shorter events, 55.3 us)
Async XLA Ops:
  11.8 25.7 %all-to-all-start = ((f32[16,16,1024]{2,1,0:T(8,128)}), f32[16,16,1024]{2,1,0:T(8,128)}, u32[]{:S(2)}, u32[]{:S(2)}) async-start(f32[16,16,1024]{2,1,0:T(8,128)} %bitcast.4), calls=%async_computation | async-start | bytes 2097152 | tf_op jit(solution)/shard_map/all_to_all | solution.py:314
  22.7 3.5 %collective-permute-start = (f32[512,256]{1,0:T(8,128)S(1)}, f32[512,256]{1,0:T(8,128)S(1)}, u32[]{:S(2)}, u32[]{:S(2)}) collective-permute-start(f32[512,256]{1,0:T(8,128)S(1)} %row_part.7), channel_id=1, source_target_pairs={{0,1},{1,0},{2,3},{3,2},{4,5},{5,4},{6,7},{7,6},{8,9},{9,8},{10,11... | collective-permute-start | bytes 1572872 | tf_op jit(solution)/shard_map/ppermute | solution.py:194
  22.8 4.8 %collective-permute-start.1 = (f32[40,1024]{1,0:T(8,128)S(1)}, f32[40,1024]{1,0:T(8,128)S(1)}, u32[]{:S(2)}, u32[]{:S(2)}) collective-permute-start(f32[40,1024]{1,0:T(8,128)S(1)} %pad_maximum_fusion.state_in), channel_id=1, source_target_pairs={{0,1},{1,2},{2,3},{3,0},{4,5},{5,6},{6,7},{7,4},{8,9},{9,10},{10,1... | collective-permute-start | bytes 491528 | tf_op jit(solution)/shard_map/ppermute | solution.py:200
  26.3 40.9 %copy-start.11 = (f32[1024]{0:T(1024)S(1)}, f32[1024]{0:T(1024)}, u32[]{:S(2)}) copy-start(f32[1024]{0:T(1024)} %param.12) | copy-start | bytes 12292
  38.8 3.8 %collective-permute-start.3 = (f32[16,1024]{1,0:T(8,128)S(1)}, f32[16,1024]{1,0:T(8,128)S(1)}, u32[]{:S(2)}, u32[]{:S(2)}) collective-permute-start(f32[16,1024]{1,0:T(8,128)S(1)} %reduce_sum.27), channel_id=1, source_target_pairs={{0,5},{1,6},{2,7},{3,4},{4,1},{5,2},{6,3},{7,0},{8,13},{9,14},{10,... | collective-permute-start | bytes 196616 | tf_op jit(solution)/shard_map/ppermute | solution.py:207
  38.8 5.1 %collective-permute-start.2 = (f32[16,1024]{1,0:T(8,128)S(1)}, f32[16,1024]{1,0:T(8,128)S(1)}, u32[]{:S(2)}, u32[]{:S(2)}) collective-permute-start(f32[16,1024]{1,0:T(8,128)S(1)} %reduce_sum.27), channel_id=1, source_target_pairs={{0,1},{1,2},{2,3},{3,0},{4,5},{5,6},{6,7},{7,4},{8,9},{9,10},{10,1... | collective-permute-start | bytes 196616 | tf_op jit(solution)/shard_map/ppermute | solution.py:200
  43.9 13.5 %collective-permute-start.4 = (f32[512,256]{1,0:T(8,128)S(1)}, f32[512,256]{1,0:T(8,128)S(1)}, u32[]{:S(2)}, u32[]{:S(2)}) collective-permute-start(f32[512,256]{1,0:T(8,128)S(1)} %add.27), channel_id=1, source_target_pairs={{0,2},{2,0},{1,3},{3,1},{4,6},{6,4},{5,7},{7,5},{8,10},{10,8},{9,1... | collective-permute-start | bytes 1572872 | tf_op jit(solution)/shard_map/ppermute | solution.py:194
  46.1 21.1 %all-to-all-start.1 = ((f32[16,16,1024]{2,1,0:T(8,128)}), f32[16,16,1024]{2,1,0:T(8,128)S(1)}, u32[]{:S(2)}, u32[]{:S(2)}) async-start(f32[16,16,1024]{2,1,0:T(8,128)} %get-tuple-element.50), calls=%async_computation.1 | async-start | bytes 2097152 | tf_op jit(solution)/shard_map/all_to_all | solution.py:327
  57.5 2.2 %collective-permute-start.5 = (f32[512,256]{1,0:T(8,128)S(1)}, f32[512,256]{1,0:T(8,128)S(1)}, u32[]{:S(2)}, u32[]{:S(2)}) collective-permute-start(f32[512,256]{1,0:T(8,128)S(1)} %add.28.mine_ref), channel_id=1, source_target_pairs={{0,1},{1,0},{2,3},{3,2},{4,5},{5,4},{6,7},{7,6},{8,9},{9,8},{10,11... | collective-permute-start | bytes 1572872 | tf_op jit(solution)/shard_map/ppermute | solution.py:194
  74.8 19.5 %all-to-all-start.2 = ((f32[16,16,1024]{2,1,0:T(8,128)}), f32[16,16,1024]{2,1,0:T(8,128)}, u32[]{:S(2)}, u32[]{:S(2)}) async-start(f32[16,16,1024]{2,1,0:T(8,128)} %bitcast.7), calls=%async_computation.2 | async-start | bytes 2097152 | tf_op jit(solution)/shard_map/all_to_all | solution.py:314
  82.2 3.6 %collective-permute-start.6 = (f32[512,256]{1,0:T(8,128)S(1)}, f32[512,256]{1,0:T(8,128)S(1)}, u32[]{:S(2)}, u32[]{:S(2)}) collective-permute-start(f32[512,256]{1,0:T(8,128)S(1)} %row_part.9), channel_id=1, source_target_pairs={{0,1},{1,0},{2,3},{3,2},{4,5},{5,4},{6,7},{7,6},{8,9},{9,8},{10,11... | collective-permute-start | bytes 1572872 | tf_op jit(solution)/shard_map/ppermute | solution.py:194
  82.3 4.8 %collective-permute-start.7 = (f32[40,1024]{1,0:T(8,128)S(1)}, f32[40,1024]{1,0:T(8,128)S(1)}, u32[]{:S(2)}, u32[]{:S(2)}) collective-permute-start(f32[40,1024]{1,0:T(8,128)S(1)} %get-tuple-element.51.state_in), channel_id=1, source_target_pairs={{0,1},{1,2},{2,3},{3,0},{4,5},{5,6},{6,7},{7,4},{8,9},{9,10},{10,1... | collective-permute-start | bytes 491528 | tf_op jit(solution)/shard_map/ppermute | solution.py:200
  95.6 3.8 %collective-permute-start.9 = (f32[16,1024]{1,0:T(8,128)S(1)}, f32[16,1024]{1,0:T(8,128)S(1)}, u32[]{:S(2)}, u32[]{:S(2)}) collective-permute-start(f32[16,1024]{1,0:T(8,128)S(1)} %reduce_sum.28), channel_id=1, source_target_pairs={{0,5},{1,6},{2,7},{3,4},{4,1},{5,2},{6,3},{7,0},{8,13},{9,14},{10,... | collective-permute-start | bytes 196616 | tf_op jit(solution)/shard_map/ppermute | solution.py:207
  95.7 3.9 %collective-permute-start.8 = (f32[16,1024]{1,0:T(8,128)S(1)}, f32[16,1024]{1,0:T(8,128)S(1)}, u32[]{:S(2)}, u32[]{:S(2)}) collective-permute-start(f32[16,1024]{1,0:T(8,128)S(1)} %reduce_sum.28), channel_id=1, source_target_pairs={{0,1},{1,2},{2,3},{3,0},{4,5},{5,6},{6,7},{7,4},{8,9},{9,10},{10,1... | collective-permute-start | bytes 196616 | tf_op jit(solution)/shard_map/ppermute | solution.py:200
  99.6 12.5 %collective-permute-start.10 = (f32[512,256]{1,0:T(8,128)S(1)}, f32[512,256]{1,0:T(8,128)S(1)}, u32[]{:S(2)}, u32[]{:S(2)}) collective-permute-start(f32[512,256]{1,0:T(8,128)S(1)} %add.29), channel_id=1, source_target_pairs={{0,2},{2,0},{1,3},{3,1},{4,6},{6,4},{5,7},{7,5},{8,10},{10,8},{9,1... | collective-permute-start | bytes 1572872 | tf_op jit(solution)/shard_map/ppermute | solution.py:194
  102.7 19.0 %all-to-all-start.3 = ((f32[16,16,1024]{2,1,0:T(8,128)}), f32[16,16,1024]{2,1,0:T(8,128)S(1)}, u32[]{:S(2)}, u32[]{:S(2)}) async-start(f32[16,16,1024]{2,1,0:T(8,128)} %get-tuple-element.62), calls=%async_computation.3 | async-start | bytes 2097152 | tf_op jit(solution)/shard_map/all_to_all | solution.py:327
  112.2 2.2 %collective-permute-start.11 = (f32[512,256]{1,0:T(8,128)S(1)}, f32[512,256]{1,0:T(8,128)S(1)}, u32[]{:S(2)}, u32[]{:S(2)}) collective-permute-start(f32[512,256]{1,0:T(8,128)S(1)} %add.30.mine_ref), channel_id=1, source_target_pairs={{0,1},{1,0},{2,3},{3,2},{4,5},{5,4},{6,7},{7,6},{8,9},{9,8},{10,11... | collective-permute-start | bytes 1572872 | tf_op jit(solution)/shard_map/ppermute | solution.py:194
  129.4 19.5 %all-to-all-start.4 = ((f32[16,16,1024]{2,1,0:T(8,128)}), f32[16,16,1024]{2,1,0:T(8,128)S(1)}, u32[]{:S(2)}, u32[]{:S(2)}) async-start(f32[16,16,1024]{2,1,0:T(8,128)} %bitcast.9), calls=%async_computation.4 | async-start | bytes 2097152 | tf_op jit(solution)/shard_map/all_to_all | solution.py:314
  136.1 3.1 %collective-permute-start.12 = (f32[512,256]{1,0:T(8,128)S(1)}, f32[512,256]{1,0:T(8,128)S(1)}, u32[]{:S(2)}, u32[]{:S(2)}) collective-permute-start(f32[512,256]{1,0:T(8,128)S(1)} %row_part.11), channel_id=1, source_target_pairs={{0,1},{1,0},{2,3},{3,2},{4,5},{5,4},{6,7},{7,6},{8,9},{9,8},{10,11... | collective-permute-start | bytes 1572872 | tf_op jit(solution)/shard_map/ppermute | solution.py:194
  139.3 39.7 %copy-start.3 = (f32[1024,256]{1,0:T(8,128)S(1)}, f32[1024,256]{1,0:T(8,128)}, u32[]{:S(2)}) copy-start(f32[1024,256]{1,0:T(8,128)} %copy-done.2) | copy-start | bytes 3145732
  149.0 5.8 %collective-permute-start.13 = (f32[16,1024]{1,0:T(8,128)S(1)}, f32[16,1024]{1,0:T(8,128)S(1)}, u32[]{:S(2)}, u32[]{:S(2)}) collective-permute-start(f32[16,1024]{1,0:T(8,128)S(1)} %reduce_sum.29.here_ref), channel_id=1, source_target_pairs={{0,4},{4,0},{1,5},{5,1},{2,6},{6,2},{3,7},{7,3},{8,12},{12,8},{9,1... | collective-permute-start | bytes 196616 | tf_op jit(solution)/shard_map/ppermute | solution.py:194
  159.8 31.4 %all-to-all-start.5 = ((f32[16,32,1024]{2,1,0:T(8,128)}), f32[16,32,1024]{2,1,0:T(8,128)S(1)}, u32[]{:S(2)}, u32[]{:S(2)}) async-start(f32[16,32,1024]{2,1,0:T(8,128)} %copy-done.4), calls=%async_computation.5 | async-start | bytes 4194304 | tf_op jit(solution)/shard_map/all_to_all | solution.py:327
  163.5 12.3 %collective-permute-start.14 = (f32[512,256]{1,0:T(8,128)}, f32[512,256]{1,0:T(8,128)S(1)}, u32[]{:S(2)}, u32[]{:S(2)}) collective-permute-start(f32[512,256]{1,0:T(8,128)} %add.31), channel_id=1, source_target_pairs={{0,2},{2,0},{1,3},{3,1},{4,6},{6,4},{5,7},{7,5},{8,10},{10,8},{9,1... | collective-permute-start | bytes 1572872 | tf_op jit(solution)/shard_map/ppermute | solution.py:194
  176.9 2.0 %collective-permute-start.15 = (f32[512,256]{1,0:T(8,128)S(1)}, f32[512,256]{1,0:T(8,128)S(1)}, u32[]{:S(2)}, u32[]{:S(2)}) collective-permute-start(f32[512,256]{1,0:T(8,128)S(1)} %add.32.mine_ref), channel_id=1, source_target_pairs={{0,1},{1,0},{2,3},{3,2},{4,5},{5,4},{6,7},{7,6},{8,9},{9,8},{10,11... | collective-permute-start | bytes 1572872 | tf_op jit(solution)/shard_map/ppermute | solution.py:194
  (10 other events, 25.5 us)

commit v4 on v3

--- a/solution.py
+++ b/solution.py
@@ -244,6 +244,27 @@
     )(here, there, state)
 
 
+def sum_kernel(terms_ref, out_ref):
+    total = terms_ref[0]
+    for n in range(1, terms_ref.shape[0]):
+        total = total + terms_ref[n]
+    out_ref[...] = total
+
+
+def summed(terms):
+    n, size, cols = terms.shape
+    wide = 2 * tile
+    return pl.pallas_call(
+        sum_kernel,
+        grid=(cols // wide,),
+        in_specs=[pl.BlockSpec((n, size, wide), lambda c: (0, 0, c))],
+        out_specs=pl.BlockSpec((size, wide), lambda c: (0, c)),
+        out_shape=jax.ShapeDtypeStruct((size, cols), f32),
+        compiler_params=pltpu.CompilerParams(vmem_limit_bytes=vmem_small),
+        name="sum",
+    )(terms)
+
+
 def row_update_kernel(scale, core_ref, mine_ref, other_ref, vecs_ref, sums_ref, vecs_out, sums_out):
     half = mine_ref.shape[0]
     for ref, n in ((mine_ref, core_ref[0]), (other_ref, 1 - core_ref[0])):
@@ -317,7 +338,7 @@
         if not last:
             state = to_next_place(state)
         terms, mine, state = lax.optimization_barrier((terms, mine, state))
-        total = jnp.sum(terms, axis=0)
+        total = summed(terms)
         if not last:
             here, there = to_next_place(total), to_next_place_and_far(total)
         else:

time: 197 us -> 196 us (level)
  local copies, waits for them, and re-layouts: 10.4 us -> 13.2 us
  starting transfers between devices: 39.2 us -> 37.1 us
    unnamed x26 -> x32, local copies, waits for them, and re-layouts: 8.01 us -> 10.9 us
    reduce_sum x3 -> x0, other arithmetic: 2.63 us -> none  [shards(): total = jnp.sum(terms, axis=0)]
  transfers between devices with their start and end apart: 22 -> 22, of which waited for: 19 -> 19; matrix products, arithmetic and copies ran while one was open for 1% -> 2% of each run, Pallas kernels for 12% -> 12%
where the time goes in v4:
time: 196 us; the launch traced here: 193 us
  waiting for transfers between devices  86.7 us (44%)
  Pallas kernels  51.6 us (26%)
  starting transfers between devices  37.1 us (19%)
  local copies, waits for them, and re-layouts  13.2 us (7%)
  other arithmetic  3.3 us (2%)
    ppermute x10, waiting for transfers between devices, swap(): return lax.ppermute(block, axis, [(i, i ^ 1) for i in range(n)])  33 us
    all_to_all x3, waiting for transfers between devices, shards(): terms = lax.all_to_all(product.reshape(n_plane, size, cols), plane, 0, 0)  25.7 us
    pallas_call x3, Pallas kernels, residual_and_product(): pl.pallas_call(functools.partial(residual_kernel, first, turn), in_specs=...  22 us
    all_to_all x3, waiting for transfers between devices, shards(): spread = lax.all_to_all(wide, plane, 0, 0)  18.5 us
    pallas_call x6, Pallas kernels, row_part_of(): pl.pallas_call(functools.partial(row_part_kernel, first), grid_spec=pltpu...  18 us
    all_to_all x3, starting transfers between devices, shards(): terms = lax.all_to_all(product.reshape(n_plane, size, cols), plane, 0, 0)  15.2 us
    all_to_all x3, starting transfers between devices, shards(): spread = lax.all_to_all(wide, plane, 0, 0)  11.1 us
    unnamed x32, local copies, waits for them, and re-layouts  10.9 us
  transfers between devices with their start and end apart: 22, of which 19 were waited for; matrix products, arithmetic and copies ran while one was open for 2% of the time, Pallas kernels for 12%

profile of v4, /device:TPU:8, one launch (start us, length us, event | category | flops | bytes accessed | tf_op | source)
XLA Modules:
  0.0 193.0 jit_solution(6560624036106272601)
XLA Ops:
  4.1 7.4 %residual.3 = (f32[256,1024]{1,0:T(8,128)S(1)}, f32[1024,1024]{1,0:T(8,128)}) custom-call(s32[3,1024,1024]{2,1,0:T(8,128)} %counts_ref.5, f32[1024,256]{1,0:T(8,128)S(1)} %copy-done.1, f32[1024,256]{1,0:T(8,128)S(1)} %copy-done, f32[8,128]{1,0:T(8,128)S(1)} %bitcast.19, f32[40,1024]{1,0:T(8,128)S(1)} %pad_maximum_fusion.state_in), custom_call_target="tpu_custom_call" | custom-call | tf_op jit(solution)/shard_map/residual/pallas_call | solution.py:118
  12.5 7.9 %all-to-all-start = ((f32[16,16,1024]{2,1,0:T(8,128)}), f32[16,16,1024]{2,1,0:T(8,128)S(1)}, u32[]{:S(2)}, u32[]{:S(2)}) async-start(f32[16,16,1024]{2,1,0:T(8,128)} %bitcast.16), calls=%async_computation | async-start | bytes 2097152 | tf_op jit(solution)/shard_map/all_to_all | solution.py:335
  28.2 9.8 %all-to-all-done.terms_ref = f32[16,16,1024]{2,1,0:T(8,128)S(1)} async-done(((f32[16,16,1024]{2,1,0:T(8,128)}), f32[16,16,1024]{2,1,0:T(8,128)S(1)}, u32[]{:S(2)}, u32[]{:S(2)}) %all-to-all-start) | async-done | bytes 1048608 | tf_op jit(solution)/shard_map/all_to_all | solution.py:335
  45.5 3.7 %all-to-all-start.1 = ((f32[16,16,1024]{2,1,0:T(8,128)}), f32[16,16,1024]{2,1,0:T(8,128)S(1)}, u32[]{:S(2)}, u32[]{:S(2)}) async-start(f32[16,16,1024]{2,1,0:T(8,128)} %get-tuple-element.50), calls=%async_computation.1 | async-start | bytes 2097152 | tf_op jit(solution)/shard_map/all_to_all | solution.py:348
  49.2 7.7 %collective-permute-done.4 = f32[512,256]{1,0:T(8,128)S(1)} collective-permute-done((f32[512,256]{1,0:T(8,128)S(1)}, f32[512,256]{1,0:T(8,128)S(1)}, u32[]{:S(2)}, u32[]{:S(2)}) %collective-permute-start.4) | collective-permute-done | bytes 524320 | tf_op jit(solution)/shard_map/ppermute | solution.py:194
  61.9 4.7 %all-to-all-done.1 = f32[16,16,1024]{2,1,0:T(8,128)S(1)} async-done(((f32[16,16,1024]{2,1,0:T(8,128)}), f32[16,16,1024]{2,1,0:T(8,128)S(1)}, u32[]{:S(2)}, u32[]{:S(2)}) %all-to-all-start.1) | async-done | bytes 1048608 | tf_op jit(solution)/shard_map/all_to_all | solution.py:348
  66.7 7.3 %residual.4 = (f32[256,1024]{1,0:T(8,128)S(1)}, f32[1024,1024]{1,0:T(8,128)}) custom-call(s32[3,1024,1024]{2,1,0:T(8,128)} %counts_ref.5, f32[1024,256]{1,0:T(8,128)S(1)} %get-tuple-element.46.row_in.vecs_ref, f32[256,1024]{1,0:T(8,128)S(1)} %bitcast.10, f32[8,128]{1,0:T(8,128)S(1)} %bitcast.20, f32[40,1024]{1,0:T(8,128)S(1)} %get-tuple-element.51.state_in), custom_call_target="tpu_custom_call" | custom-call | tf_op jit(solution)/shard_map/residual/pallas_call | solution.py:118
  75.0 3.7 %all-to-all-start.2 = ((f32[16,16,1024]{2,1,0:T(8,128)}), f32[16,16,1024]{2,1,0:T(8,128)S(1)}, u32[]{:S(2)}, u32[]{:S(2)}) async-start(f32[16,16,1024]{2,1,0:T(8,128)} %bitcast.17), calls=%async_computation.2 | async-start | bytes 2097152 | tf_op jit(solution)/shard_map/all_to_all | solution.py:335
  78.6 3.0 %row_part.9 = f32[512,256]{1,0:T(8,128)S(1)} custom-call(s32[1]{0:T(128)} %bitcast.5.half_ref, f32[1024,1024]{1,0:T(8,128)} %get-tuple-element.53.residual_ref, f32[256,1024]{1,0:T(8,128)S(1)} %bitcast.11), custom_call_target="tpu_custom_call" | custom-call | tf_op jit(solution)/shard_map/row_part/pallas_call | solution.py:168
  86.6 7.2 %all-to-all-done.2.terms_ref = f32[16,16,1024]{2,1,0:T(8,128)S(1)} async-done(((f32[16,16,1024]{2,1,0:T(8,128)}), f32[16,16,1024]{2,1,0:T(8,128)S(1)}, u32[]{:S(2)}, u32[]{:S(2)}) %all-to-all-start.2) | async-done | bytes 1048608 | tf_op jit(solution)/shard_map/all_to_all | solution.py:335
  94.5 3.3 %collective-permute-done.9.there_ref = f32[16,1024]{1,0:T(8,128)S(1)} collective-permute-done((f32[16,1024]{1,0:T(8,128)S(1)}, f32[16,1024]{1,0:T(8,128)S(1)}, u32[]{:S(2)}, u32[]{:S(2)}) %collective-permute-start.9) | collective-permute-done | bytes 65568 | tf_op jit(solution)/shard_map/ppermute | solution.py:207
  101.1 3.7 %all-to-all-start.3 = ((f32[16,16,1024]{2,1,0:T(8,128)}), f32[16,16,1024]{2,1,0:T(8,128)S(1)}, u32[]{:S(2)}, u32[]{:S(2)}) async-start(f32[16,16,1024]{2,1,0:T(8,128)} %get-tuple-element.62), calls=%async_computation.3 | async-start | bytes 2097152 | tf_op jit(solution)/shard_map/all_to_all | solution.py:348
  104.8 5.9 %collective-permute-done.10 = f32[512,256]{1,0:T(8,128)} collective-permute-done((f32[512,256]{1,0:T(8,128)S(1)}, f32[512,256]{1,0:T(8,128)}, u32[]{:S(2)}, u32[]{:S(2)}) %collective-permute-start.10) | collective-permute-done | bytes 524320 | tf_op jit(solution)/shard_map/ppermute | solution.py:194
  116.8 4.0 %all-to-all-done.3 = f32[16,16,1024]{2,1,0:T(8,128)S(1)} async-done(((f32[16,16,1024]{2,1,0:T(8,128)}), f32[16,16,1024]{2,1,0:T(8,128)S(1)}, u32[]{:S(2)}, u32[]{:S(2)}) %all-to-all-start.3) | async-done | bytes 1048608 | tf_op jit(solution)/shard_map/all_to_all | solution.py:348
  120.7 7.3 %residual.5 = (f32[256,1024]{1,0:T(8,128)S(1)}, f32[1024,1024]{1,0:T(8,128)}) custom-call(s32[3,1024,1024]{2,1,0:T(8,128)} %counts_ref.5, f32[1024,256]{1,0:T(8,128)S(1)} %get-tuple-element.58.row_in.vecs_ref, f32[256,1024]{1,0:T(8,128)S(1)} %bitcast.13, f32[8,128]{1,0:T(8,128)S(1)} %bitcast.21, f32[40,1024]{1,0:T(8,128)S(1)} %get-tuple-element.74.state_in.state_ref), custom_call_target="tpu_custom_call" | custom-call | tf_op jit(solution)/shard_map/residual/pallas_call | solution.py:118
  129.1 3.7 %all-to-all-start.4 = ((f32[16,16,1024]{2,1,0:T(8,128)}), f32[16,16,1024]{2,1,0:T(8,128)S(1)}, u32[]{:S(2)}, u32[]{:S(2)}) async-start(f32[16,16,1024]{2,1,0:T(8,128)} %bitcast.18), calls=%async_computation.4 | async-start | bytes 2097152 | tf_op jit(solution)/shard_map/all_to_all | solution.py:335
  132.7 3.0 %row_part.11 = f32[512,256]{1,0:T(8,128)S(1)} custom-call(s32[1]{0:T(128)} %bitcast.5.half_ref, f32[1024,1024]{1,0:T(8,128)} %get-tuple-element.65.residual_ref, f32[256,1024]{1,0:T(8,128)S(1)} %bitcast.14), custom_call_target="tpu_custom_call" | custom-call | tf_op jit(solution)/shard_map/row_part/pallas_call | solution.py:168
  135.9 3.0 %row_part.10 = f32[512,256]{1,0:T(8,128)S(1)} custom-call(s32[1]{0:T(128)} %bitcast.half_ref.core_ref, f32[1024,1024]{1,0:T(8,128)} %get-tuple-element.65.residual_ref, f32[256,1024]{1,0:T(8,128)S(1)} %bitcast.15), custom_call_target="tpu_custom_call" | custom-call | tf_op jit(solution)/shard_map/row_part/pallas_call | solution.py:168
  139.8 8.7 %all-to-all-done.4.terms_ref = f32[16,16,1024]{2,1,0:T(8,128)S(1)} async-done(((f32[16,16,1024]{2,1,0:T(8,128)}), f32[16,16,1024]{2,1,0:T(8,128)S(1)}, u32[]{:S(2)}, u32[]{:S(2)}) %all-to-all-start.4) | async-done | bytes 1048608 | tf_op jit(solution)/shard_map/all_to_all | solution.py:335
  150.2 4.3 %collective-permute-done.13.there_ref = f32[16,1024]{1,0:T(8,128)S(1)} collective-permute-done((f32[16,1024]{1,0:T(8,128)S(1)}, f32[16,1024]{1,0:T(8,128)S(1)}, u32[]{:S(2)}, u32[]{:S(2)}) %collective-permute-start.13) | collective-permute-done | bytes 65568 | tf_op jit(solution)/shard_map/ppermute | solution.py:194
  154.5 3.6 %update.5 = (f32[16,32,1024]{2,1,0:T(8,128)S(1)}, f32[40,1024]{1,0:T(8,128)}) custom-call(f32[16,1024]{1,0:T(8,128)S(1)} %sum.5.here_ref, f32[16,1024]{1,0:T(8,128)S(1)} %collective-permute-done.13.there_ref, f32[40,1024]{1,0:T(8,128)S(1)} %get-tuple-element.74.state_in.state_ref), custom_call_target="tpu_custom_call" | custom-call | tf_op jit(solution)/shard_map/update/pallas_call | solution.py:233
  159.4 3.7 %all-to-all-start.5 = ((f32[16,32,1024]{2,1,0:T(8,128)}), f32[16,32,1024]{2,1,0:T(8,128)S(1)}, u32[]{:S(2)}, u32[]{:S(2)}) async-start(f32[16,32,1024]{2,1,0:T(8,128)} %copy-done.4), calls=%async_computation.5 | async-start | bytes 4194304 | tf_op jit(solution)/shard_map/all_to_all | solution.py:348
  165.4 9.4 %collective-permute-done.14 = f32[512,256]{1,0:T(8,128)S(1)} collective-permute-done((f32[512,256]{1,0:T(8,128)}, f32[512,256]{1,0:T(8,128)S(1)}, u32[]{:S(2)}, u32[]{:S(2)}) %collective-permute-start.14) | collective-permute-done | bytes 524320 | tf_op jit(solution)/shard_map/ppermute | solution.py:194
  181.0 9.8 %all-to-all-done.5.spread_ref = f32[16,32,1024]{2,1,0:T(8,128)S(1)} async-done(((f32[16,32,1024]{2,1,0:T(8,128)}), f32[16,32,1024]{2,1,0:T(8,128)S(1)}, u32[]{:S(2)}, u32[]{:S(2)}) %all-to-all-start.5) | async-done | bytes 2097184 | tf_op jit(solution)/shard_map/all_to_all | solution.py:348
  (80 shorter events, 56.2 us)
Async XLA Ops:
  12.5 25.5 %all-to-all-start = ((f32[16,16,1024]{2,1,0:T(8,128)}), f32[16,16,1024]{2,1,0:T(8,128)S(1)}, u32[]{:S(2)}, u32[]{:S(2)}) async-start(f32[16,16,1024]{2,1,0:T(8,128)} %bitcast.16), calls=%async_computation | async-start | bytes 2097152 | tf_op jit(solution)/shard_map/all_to_all | solution.py:335
  23.3 3.5 %collective-permute-start = (f32[512,256]{1,0:T(8,128)S(1)}, f32[512,256]{1,0:T(8,128)S(1)}, u32[]{:S(2)}, u32[]{:S(2)}) collective-permute-start(f32[512,256]{1,0:T(8,128)S(1)} %row_part.7), channel_id=1, source_target_pairs={{0,1},{1,0},{2,3},{3,2},{4,5},{5,4},{6,7},{7,6},{8,9},{9,8},{10,11... | collective-permute-start | bytes 1572872 | tf_op jit(solution)/shard_map/ppermute | solution.py:194
  23.4 4.8 %collective-permute-start.1 = (f32[40,1024]{1,0:T(8,128)S(1)}, f32[40,1024]{1,0:T(8,128)S(1)}, u32[]{:S(2)}, u32[]{:S(2)}) collective-permute-start(f32[40,1024]{1,0:T(8,128)S(1)} %pad_maximum_fusion.state_in), channel_id=1, source_target_pairs={{0,1},{1,2},{2,3},{3,0},{4,5},{5,6},{6,7},{7,4},{8,9},{9,10},{10,1... | collective-permute-start | bytes 491528 | tf_op jit(solution)/shard_map/ppermute | solution.py:200
  26.9 39.7 %copy-start.14 = (f32[1024]{0:T(1024)S(1)}, f32[1024]{0:T(1024)}, u32[]{:S(2)}) copy-start(f32[1024]{0:T(1024)} %param.12) | copy-start | bytes 12292
  38.2 3.8 %collective-permute-start.3 = (f32[16,1024]{1,0:T(8,128)S(1)}, f32[16,1024]{1,0:T(8,128)S(1)}, u32[]{:S(2)}, u32[]{:S(2)}) collective-permute-start(f32[16,1024]{1,0:T(8,128)S(1)} %sum.3), channel_id=1, source_target_pairs={{0,5},{1,6},{2,7},{3,4},{4,1},{5,2},{6,3},{7,0},{8,13},{9,14},{10,... | collective-permute-start | bytes 196616 | tf_op jit(solution)/shard_map/ppermute | solution.py:207
  38.3 5.1 %collective-permute-start.2 = (f32[16,1024]{1,0:T(8,128)S(1)}, f32[16,1024]{1,0:T(8,128)S(1)}, u32[]{:S(2)}, u32[]{:S(2)}) collective-permute-start(f32[16,1024]{1,0:T(8,128)S(1)} %sum.3), channel_id=1, source_target_pairs={{0,1},{1,2},{2,3},{3,0},{4,5},{5,6},{6,7},{7,4},{8,9},{9,10},{10,1... | collective-permute-start | bytes 196616 | tf_op jit(solution)/shard_map/ppermute | solution.py:200
  43.4 13.5 %collective-permute-start.4 = (f32[512,256]{1,0:T(8,128)S(1)}, f32[512,256]{1,0:T(8,128)S(1)}, u32[]{:S(2)}, u32[]{:S(2)}) collective-permute-start(f32[512,256]{1,0:T(8,128)S(1)} %add.27), channel_id=1, source_target_pairs={{0,2},{2,0},{1,3},{3,1},{4,6},{6,4},{5,7},{7,5},{8,10},{10,8},{9,1... | collective-permute-start | bytes 1572872 | tf_op jit(solution)/shard_map/ppermute | solution.py:194
  45.5 21.1 %all-to-all-start.1 = ((f32[16,16,1024]{2,1,0:T(8,128)}), f32[16,16,1024]{2,1,0:T(8,128)S(1)}, u32[]{:S(2)}, u32[]{:S(2)}) async-start(f32[16,16,1024]{2,1,0:T(8,128)} %get-tuple-element.50), calls=%async_computation.1 | async-start | bytes 2097152 | tf_op jit(solution)/shard_map/all_to_all | solution.py:348
  57.0 2.2 %collective-permute-start.5 = (f32[512,256]{1,0:T(8,128)S(1)}, f32[512,256]{1,0:T(8,128)S(1)}, u32[]{:S(2)}, u32[]{:S(2)}) collective-permute-start(f32[512,256]{1,0:T(8,128)S(1)} %add.28.mine_ref), channel_id=1, source_target_pairs={{0,1},{1,0},{2,3},{3,2},{4,5},{5,4},{6,7},{7,6},{8,9},{9,8},{10,11... | collective-permute-start | bytes 1572872 | tf_op jit(solution)/shard_map/ppermute | solution.py:194
  75.0 18.8 %all-to-all-start.2 = ((f32[16,16,1024]{2,1,0:T(8,128)}), f32[16,16,1024]{2,1,0:T(8,128)S(1)}, u32[]{:S(2)}, u32[]{:S(2)}) async-start(f32[16,16,1024]{2,1,0:T(8,128)} %bitcast.17), calls=%async_computation.2 | async-start | bytes 2097152 | tf_op jit(solution)/shard_map/all_to_all | solution.py:335
  81.7 3.6 %collective-permute-start.6 = (f32[512,256]{1,0:T(8,128)S(1)}, f32[512,256]{1,0:T(8,128)S(1)}, u32[]{:S(2)}, u32[]{:S(2)}) collective-permute-start(f32[512,256]{1,0:T(8,128)S(1)} %row_part.9), channel_id=1, source_target_pairs={{0,1},{1,0},{2,3},{3,2},{4,5},{5,4},{6,7},{7,6},{8,9},{9,8},{10,11... | collective-permute-start | bytes 1572872 | tf_op jit(solution)/shard_map/ppermute | solution.py:194
  81.8 4.8 %collective-permute-start.7 = (f32[40,1024]{1,0:T(8,128)S(1)}, f32[40,1024]{1,0:T(8,128)S(1)}, u32[]{:S(2)}, u32[]{:S(2)}) collective-permute-start(f32[40,1024]{1,0:T(8,128)S(1)} %get-tuple-element.51.state_in), channel_id=1, source_target_pairs={{0,1},{1,2},{2,3},{3,0},{4,5},{5,6},{6,7},{7,4},{8,9},{9,10},{10,1... | collective-permute-start | bytes 491528 | tf_op jit(solution)/shard_map/ppermute | solution.py:200
  94.0 3.8 %collective-permute-start.9 = (f32[16,1024]{1,0:T(8,128)S(1)}, f32[16,1024]{1,0:T(8,128)S(1)}, u32[]{:S(2)}, u32[]{:S(2)}) collective-permute-start(f32[16,1024]{1,0:T(8,128)S(1)} %sum.4), channel_id=1, source_target_pairs={{0,5},{1,6},{2,7},{3,4},{4,1},{5,2},{6,3},{7,0},{8,13},{9,14},{10,... | collective-permute-start | bytes 196616 | tf_op jit(solution)/shard_map/ppermute | solution.py:207
  94.1 3.9 %collective-permute-start.8 = (f32[16,1024]{1,0:T(8,128)S(1)}, f32[16,1024]{1,0:T(8,128)S(1)}, u32[]{:S(2)}, u32[]{:S(2)}) collective-permute-start(f32[16,1024]{1,0:T(8,128)S(1)} %sum.4), channel_id=1, source_target_pairs={{0,1},{1,2},{2,3},{3,0},{4,5},{5,6},{6,7},{7,4},{8,9},{9,10},{10,1... | collective-permute-start | bytes 196616 | tf_op jit(solution)/shard_map/ppermute | solution.py:200
  98.0 12.7 %collective-permute-start.10 = (f32[512,256]{1,0:T(8,128)S(1)}, f32[512,256]{1,0:T(8,128)}, u32[]{:S(2)}, u32[]{:S(2)}) collective-permute-start(f32[512,256]{1,0:T(8,128)S(1)} %add.29), channel_id=1, source_target_pairs={{0,2},{2,0},{1,3},{3,1},{4,6},{6,4},{5,7},{7,5},{8,10},{10,8},{9,1... | collective-permute-start | bytes 1572872 | tf_op jit(solution)/shard_map/ppermute | solution.py:194
  101.1 19.6 %all-to-all-start.3 = ((f32[16,16,1024]{2,1,0:T(8,128)}), f32[16,16,1024]{2,1,0:T(8,128)S(1)}, u32[]{:S(2)}, u32[]{:S(2)}) async-start(f32[16,16,1024]{2,1,0:T(8,128)} %get-tuple-element.62), calls=%async_computation.3 | async-start | bytes 2097152 | tf_op jit(solution)/shard_map/all_to_all | solution.py:348
  111.8 2.2 %collective-permute-start.11 = (f32[512,256]{1,0:T(8,128)S(1)}, f32[512,256]{1,0:T(8,128)S(1)}, u32[]{:S(2)}, u32[]{:S(2)}) collective-permute-start(f32[512,256]{1,0:T(8,128)S(1)} %add.30.mine_ref), channel_id=1, source_target_pairs={{0,1},{1,0},{2,3},{3,2},{4,5},{5,4},{6,7},{7,6},{8,9},{9,8},{10,11... | collective-permute-start | bytes 1572872 | tf_op jit(solution)/shard_map/ppermute | solution.py:194
  129.1 19.4 %all-to-all-start.4 = ((f32[16,16,1024]{2,1,0:T(8,128)}), f32[16,16,1024]{2,1,0:T(8,128)S(1)}, u32[]{:S(2)}, u32[]{:S(2)}) async-start(f32[16,16,1024]{2,1,0:T(8,128)} %bitcast.18), calls=%async_computation.4 | async-start | bytes 2097152 | tf_op jit(solution)/shard_map/all_to_all | solution.py:335
  135.8 3.1 %collective-permute-start.12 = (f32[512,256]{1,0:T(8,128)S(1)}, f32[512,256]{1,0:T(8,128)S(1)}, u32[]{:S(2)}, u32[]{:S(2)}) collective-permute-start(f32[512,256]{1,0:T(8,128)S(1)} %row_part.11), channel_id=1, source_target_pairs={{0,1},{1,0},{2,3},{3,2},{4,5},{5,4},{6,7},{7,6},{8,9},{9,8},{10,11... | collective-permute-start | bytes 1572872 | tf_op jit(solution)/shard_map/ppermute | solution.py:194
  138.9 39.0 %copy-start.3 = (f32[1024,256]{1,0:T(8,128)S(1)}, f32[1024,256]{1,0:T(8,128)}, u32[]{:S(2)}) copy-start(f32[1024,256]{1,0:T(8,128)} %copy-done.2) | copy-start | bytes 3145732
  148.7 5.8 %collective-permute-start.13 = (f32[16,1024]{1,0:T(8,128)S(1)}, f32[16,1024]{1,0:T(8,128)S(1)}, u32[]{:S(2)}, u32[]{:S(2)}) collective-permute-start(f32[16,1024]{1,0:T(8,128)S(1)} %sum.5.here_ref), channel_id=1, source_target_pairs={{0,4},{4,0},{1,5},{5,1},{2,6},{6,2},{3,7},{7,3},{8,12},{12,8},{9,1... | collective-permute-start | bytes 196616 | tf_op jit(solution)/shard_map/ppermute | solution.py:194
  159.4 31.4 %all-to-all-start.5 = ((f32[16,32,1024]{2,1,0:T(8,128)}), f32[16,32,1024]{2,1,0:T(8,128)S(1)}, u32[]{:S(2)}, u32[]{:S(2)}) async-start(f32[16,32,1024]{2,1,0:T(8,128)} %copy-done.4), calls=%async_computation.5 | async-start | bytes 4194304 | tf_op jit(solution)/shard_map/all_to_all | solution.py:348
  163.2 11.6 %collective-permute-start.14 = (f32[512,256]{1,0:T(8,128)}, f32[512,256]{1,0:T(8,128)S(1)}, u32[]{:S(2)}, u32[]{:S(2)}) collective-permute-start(f32[512,256]{1,0:T(8,128)} %add.31), channel_id=1, source_target_pairs={{0,2},{2,0},{1,3},{3,1},{4,6},{6,4},{5,7},{7,5},{8,10},{10,8},{9,1... | collective-permute-start | bytes 1572872 | tf_op jit(solution)/shard_map/ppermute | solution.py:194
  175.9 2.0 %collective-permute-start.15 = (f32[512,256]{1,0:T(8,128)S(1)}, f32[512,256]{1,0:T(8,128)S(1)}, u32[]{:S(2)}, u32[]{:S(2)}) collective-permute-start(f32[512,256]{1,0:T(8,128)S(1)} %add.32.mine_ref), channel_id=1, source_target_pairs={{0,1},{1,0},{2,3},{3,2},{4,5},{5,4},{6,7},{7,6},{8,9},{9,8},{10,11... | collective-permute-start | bytes 1572872 | tf_op jit(solution)/shard_map/ppermute | solution.py:194
  (13 other events, 27.4 us)
